TPU v7x, 256 devices: a whole 4x4x8 slice. The times are simulated.
256 devices in a mesh: space: 8 (over x_hi, y), tm: 32 (over x_lo, z, core).
Axes of the slice: x: 4 (x_hi: 2, x_lo: 2; x = x_hi * 2 + x_lo), y: 4, z: 8, core: 2. Of those that a mesh axis runs over, the one named last changes fastest.
Arguments:
- initial_guess: float32 [4, 256, 64, 4, 128], P(None, 'tm', 'space'), may hold values from -6 to 6
- forcing: float32 [4, 256, 64, 4, 128], P(None, 'tm', 'space'), may hold values from -6 to 6
- visc_table: float32 [8], replicated, may hold values from 0.05 to 0.5
- visc_class: int32 [64, 4, 128], P('space'), may hold values from 0 to 7
- inverse_bank: bfloat16 [4, 32, 32], replicated, may hold values from -0.125 to 0.125
- patch_kind: int32 [32, 2, 64], P('space'), may hold values from 0 to 3
Outputs:
- smoothed: float32 [4, 256, 64, 4, 128], P(None, 'tm', 'space')
- coarse: float32 [4, 8, 32768], P(None, None, ('space', 'tm'))
All inputs are finite; a program needn't handle non-finite values.
Results may differ from a plain program's by a relative error of at most 0.00096.
Values sent between devices are 32-bit elements; how exact they have to be, the bound alone decides.
A program may use at most 64 MiB of HBM per device.

v0:
```python
import jax
import jax.numpy as jnp
from jax import lax
from jax.sharding import PartitionSpec as P

SWEEPS = 2
LEVELS = 5


damping = 0.8
mass_weight = 1.0
stabilize = 0.1


def extended_2(shard, sides, width):
    for axis, dim in sides:
        size, length = (lax.axis_size(axis), shard.shape[dim])
        up = [(i, (i + 1) % size) for i in range(size - 1)]
        down = [(j, i) for i, j in up]
        last = lax.slice_in_dim(shard, length - width, length, axis=dim)
        leading = lax.slice_in_dim(shard, 0, width, axis=dim)
        before = lax.ppermute(last, axis, up)
        after = lax.ppermute(leading, axis, down)
        shard = jnp.concatenate([before, shard, after], axis=dim)
    return shard


def passed_along(shard, axis, by):
    length = lax.axis_size(axis)
    pairs = [(i, i + by) for i in range(length) if 0 <= i + by < length]
    return lax.ppermute(shard, axis, pairs)


def neighbour(array, offset):
    size_x = array.shape[-3] - 2
    size_y = array.shape[-2] - 2
    size_z = array.shape[-1] - 2
    return array[
        ...,
        1 + offset[0] : 1 + offset[0] + size_x,
        1 + offset[1] : 1 + offset[1] + size_y,
        1 + offset[2] : 1 + offset[2] + size_z,
    ]


def operate(padded, earlier, visc_pad):
    extended = jnp.pad(padded, ((0, 0), (0, 0), (0, 0), (1, 1), (1, 1)))
    viscous = jnp.pad(visc_pad, ((0, 0), (1, 1), (1, 1)))
    centre = (0, 0, 0)
    centre_visc = neighbour(viscous, centre)
    velocity = neighbour(extended[:3], centre)
    pressure = neighbour(extended[3], centre)
    units = ((1, 0, 0), (0, 1, 0), (0, 0, 1))
    diffusion = jnp.zeros_like(velocity)
    pressure_sum = jnp.zeros_like(pressure)
    gradient = []
    divergence = jnp.zeros_like(pressure)
    for number in range(3):
        unit = units[number]
        minus = (-unit[0], -unit[1], -unit[2])
        for offset in (unit, minus):
            kappa = 0.5 * (centre_visc + neighbour(viscous, offset))
            diffusion = diffusion + kappa * (velocity - neighbour(extended[:3], offset))
            pressure_sum = pressure_sum + neighbour(extended[3], offset)
        gradient.append(0.5 * (neighbour(extended[3], unit) - neighbour(extended[3], minus)))
        divergence = divergence + 0.5 * (
            neighbour(extended[number], unit) - neighbour(extended[number], minus)
        )
    previous = jnp.concatenate([earlier[:, None], velocity[:, :-1]], axis=1)
    momentum = mass_weight * (velocity - previous) + diffusion + jnp.stack(gradient)
    continuity = stabilize * (6.0 * pressure - pressure_sum) - divergence
    return jnp.concatenate([momentum, continuity[None]], axis=0)


def lookup(classes, table):
    labels = jnp.arange(table.shape[0], dtype=jnp.int32).reshape(-1, 1, 1, 1)
    return jnp.sum(jnp.where(classes[None] == labels, table.reshape(-1, 1, 1, 1), 0.0), axis=0)


def vanka_patches(resid, inverse_bank, patch_kind):
    kinds_count = inverse_bank.shape[0]
    comps, steps, size_x, size_y, size_z = resid.shape
    pairs_x = size_x // 2
    quads_y = size_y // 4
    half_z = size_z // 2
    side_x = jnp.arange(2, dtype=jnp.int32).reshape(2, 1, 1)
    row_y = jnp.arange(4, dtype=jnp.int32).reshape(1, 4, 1)
    cell_z = jnp.arange(size_z, dtype=jnp.int32).reshape(1, 1, size_z)
    parity = 4 * side_x + 2 * (row_y % 2) + cell_z % 2
    column = parity * size_z + row_y // 2 * half_z + cell_z // 2
    targets = jnp.arange(8 * size_z, dtype=jnp.int32)
    permuter = (column[..., None] == targets).astype(jnp.bfloat16)
    blocks = resid.astype(jnp.bfloat16).reshape(comps, steps, pairs_x, 2, quads_y, 4, size_z)
    grouped = lax.dot_general(
        blocks, permuter, (((3, 5, 6), (0, 1, 2)), ((), ())), preferred_element_type=jnp.float32
    )
    grouped = grouped.astype(jnp.bfloat16).reshape(comps, steps, pairs_x, quads_y, 8, size_z)
    bank_flat = inverse_bank.reshape(kinds_count * 8 * comps, comps, 8)
    products = lax.dot_general(
        bank_flat, grouped, (((1, 2), (0, 4)), ((), ())), preferred_element_type=jnp.float32
    )
    products = products.reshape(kinds_count, comps, 8, steps, pairs_x, quads_y, size_z)
    kinds_flat = patch_kind.reshape(pairs_x, quads_y, size_z)
    labels = jnp.arange(kinds_count, dtype=jnp.int32).reshape(-1, 1, 1, 1, 1, 1, 1)
    chosen = jnp.sum(jnp.where(kinds_flat[None, None, None, None] == labels, products, 0.0), axis=0)
    scaled = damping * chosen
    back_table = permuter.astype(jnp.float32).reshape(2, 4, size_z, 8, size_z)
    placed = lax.dot_general(
        scaled,
        back_table,
        (((1, 5), (3, 4)), ((), ())),
        precision=lax.Precision.HIGHEST,
        preferred_element_type=jnp.float32,
    )
    placed = placed.transpose(0, 1, 2, 4, 3, 5, 6)
    return placed.reshape(comps, steps, size_x, size_y, size_z)


def coarsen(level_now, before_step):
    even_steps = level_now[:, 0::2]
    odd_steps = level_now[:, 1::2]
    shifted = jnp.concatenate([before_step[:, None], odd_steps[:, :-1]], axis=1)
    return 0.25 * shifted + 0.5 * even_steps + 0.25 * odd_steps


def per_device(initial_guess, forcing, visc_table, visc_class, inverse_bank, patch_kind):
    viscosity = lookup(visc_class, visc_table)
    visc_pad = extended_2(viscosity, (("space", 0),), 1)

    def residual_of(iterate):
        padded = extended_2(iterate, (("space", 2),), 1)
        earlier = passed_along(iterate[:3, -1], "tm", 1)
        return forcing - operate(padded, earlier, visc_pad)

    iterate = initial_guess
    for sweep_index in range(SWEEPS):
        iterate = iterate + vanka_patches(residual_of(iterate), inverse_bank, patch_kind)
    final = residual_of(iterate)
    flattened = final.reshape(final.shape[0], final.shape[1], -1)
    result = lax.all_to_all(flattened, "tm", split_axis=2, concat_axis=1, tiled=True)
    for level_index in range(LEVELS):
        result = coarsen(result, jnp.zeros_like(result[:, 0]))
    return (iterate, result)


def solution(mesh):
    return jax.shard_map(
        per_device,
        mesh=mesh,
        in_specs=(
            P(None, "tm", "space", None, None),
            P(None, "tm", "space", None, None),
            P(),
            P("space", None, None),
            P(),
            P("space", None, None),
        ),
        out_specs=(P(None, "tm", "space", None, None), P(None, None, ("space", "tm"))),
        check_vma=False,
    )
```

profile of v0, /device:TPU:5, one launch (start us, length us, event | category | flops | bytes accessed | tf_op | source)
XLA Modules:
  0.0 141.9 jit_solution(4981324915584095697)
XLA Ops:
  0.6 0.9 fusion.133
  1.5 4.6 %collective-permute-start.2 = (f32[4,8,1,4,128]{4,3,2,1,0:T(4,128)S(1)}, f32[4,8,1,4,128]{4,3,2,1,0:T(4,128)S(1)}, u32[]{:S(2)}, u32[]{:S(2)}) collective-permute-start(f32[4,8,1,4,128]{4,3,2,1,0:T(4,128)S(1)} %get-tuple-element.31), channel_id=1, source_target_pairs={{32,0},{64,32},{96,64},{128,96},{160,128},{192,160},{224,192},{33,... | collective-permute-start | bytes 196616 | tf_op jit(solution)/shard_map/ppermute | solution.py:23
  6.1 1.9 %collective-permute-start.4 = (f32[4,8,1,4,128]{4,3,2,1,0:T(4,128)S(1)}, f32[4,8,1,4,128]{4,3,2,1,0:T(4,128)S(1)}, u32[]{:S(2)}, u32[]{:S(2)}) collective-permute-start(f32[4,8,1,4,128]{4,3,2,1,0:T(4,128)S(1)} %get-tuple-element.30), channel_id=1, source_target_pairs={{0,32},{32,64},{64,96},{96,128},{128,160},{160,192},{192,224},{1,3... | collective-permute-start | bytes 196616 | tf_op jit(solution)/shard_map/ppermute | solution.py:22
  8.0 0.7 copy.25
  8.8 0.7 select_reduce_fusion
  9.5 7.0 %collective-permute-start.1 = (f32[1,4,128]{2,0,1:T(1,128)S(1)}, f32[1,4,128]{2,0,1:T(1,128)S(1)}, u32[]{:S(2)}, u32[]{:S(2)}) collective-permute-start(f32[1,4,128]{2,0,1:T(1,128)S(1)} %get-tuple-element.39), channel_id=1, source_target_pairs={{32,0},{64,32},{96,64},{128,96},{160,128},{192,160},{224,192},{33,... | collective-permute-start | bytes 6152 | tf_op jit(solution)/shard_map/ppermute | solution.py:23
  16.5 1.9 %collective-permute-start.3 = (f32[1,4,128]{2,0,1:T(1,128)S(1)}, f32[1,4,128]{2,0,1:T(1,128)S(1)}, u32[]{:S(2)}, u32[]{:S(2)}) collective-permute-start(f32[1,4,128]{2,0,1:T(1,128)S(1)} %get-tuple-element.38), channel_id=1, source_target_pairs={{0,32},{32,64},{64,96},{96,128},{128,160},{160,192},{192,224},{1,3... | collective-permute-start | bytes 6152 | tf_op jit(solution)/shard_map/ppermute | solution.py:22
  18.4 0.8 slice_bitcast_fusion.14
  19.2 4.9 %collective-permute-start = (f32[3,8,4,128]{3,2,1,0:T(4,128)S(1)}, f32[3,8,4,128]{3,2,1,0:T(4,128)S(1)}, u32[]{:S(2)}, u32[]{:S(2)}) collective-permute-start(f32[3,8,4,128]{3,2,1,0:T(4,128)S(1)} %slice_bitcast_fusion.14), channel_id=1, source_target_pairs={{0,1},{1,2},{2,3},{3,4},{4,5},{5,6},{6,7},{7,8},{8,9},{9,10},{10,1... | collective-permute-start | bytes 147464 | tf_op jit(solution)/shard_map/ppermute | solution.py:31
  24.2 0.8 eq.95
  25.2 1.0 slice.472
  26.2 0.9 dot_general.25
  27.4 1.8 %select_maximum_fusion.4 = f32[4,8,10,6,130]{4,3,2,1,0:T(8,128)S(1)} fusion(f32[4,8,1,4,128]{4,3,2,1,0:T(4,128)S(1)} %collective-permute-done.2, f32[4,8,8,4,128]{4,3,2,1,0:T(4,128)} %param.6, f32[4,8,1,4,128]{4,3,2,1,0:T(4,128)S(1)} %collective-permute-done.4), kind=kLoop, calls=%fused_computation.18 | loop fusion | flops 3744000 | bytes 1653760 | tf_op jit(solution)/shard_map/concatenate | solution.py:24
  29.2 0.2 slice_bitcast_fusion.11
  29.4 0.8 multiply_bitcast_fusion.8
  30.2 1.0 fusion.79
  31.2 0.2 fusion.40
  31.4 1.0 fusion.34
  32.5 0.5 fusion.15
  32.9 2.5 %fusion.7 = f32[4,8,4,2,4,128,1]{5,1,6,4,3,2,0:T(8,128)S(1)} fusion(s32[8,128]{1,0:T(8,128)S(1)} %multiply_add_fusion.5, s32[2,4,128]{2,1,0:T(4,128)S(1)} %add_add_fusion, f32[4,8,8,4,128]{4,1,0,3,2:T(8,128)S(1)} %fusion.15), kind=kOutput, calls=%fused_computation.6 | convolution fusion | flops 1611792384 | bytes 1056768 | tf_op jit(solution)/shard_map/dot_general | solution.py:108
  35.5 0.2 copy_add_fusion.1
  35.7 7.3 %collective-permute-start.6 = (f32[4,8,1,4,128]{4,3,2,1,0:T(4,128)S(1)}, f32[4,8,1,4,128]{4,3,2,1,0:T(4,128)S(1)}, u32[]{:S(2)}, u32[]{:S(2)}) collective-permute-start(f32[4,8,1,4,128]{4,3,2,1,0:T(4,128)S(1)} %get-tuple-element.29), channel_id=1, source_target_pairs={{32,0},{64,32},{96,64},{128,96},{160,128},{192,160},{224,192},{33,... | collective-permute-start | bytes 196616 | tf_op jit(solution)/shard_map/ppermute | solution.py:23
  43.0 1.9 %collective-permute-start.7 = (f32[4,8,1,4,128]{4,3,2,1,0:T(4,128)S(1)}, f32[4,8,1,4,128]{4,3,2,1,0:T(4,128)S(1)}, u32[]{:S(2)}, u32[]{:S(2)}) collective-permute-start(f32[4,8,1,4,128]{4,3,2,1,0:T(4,128)S(1)} %get-tuple-element.28), channel_id=1, source_target_pairs={{0,32},{32,64},{64,96},{96,128},{128,160},{160,192},{192,224},{1,3... | collective-permute-start | bytes 196616 | tf_op jit(solution)/shard_map/ppermute | solution.py:22
  44.9 2.4 %collective-permute-start.5 = (f32[3,8,4,128]{3,2,1,0:T(4,128)S(1)}, f32[3,8,4,128]{3,2,1,0:T(4,128)S(1)}, u32[]{:S(2)}, u32[]{:S(2)}) collective-permute-start(f32[3,8,4,128]{3,2,1,0:T(4,128)S(1)} %slice_bitcast_fusion.13), channel_id=1, source_target_pairs={{0,1},{1,2},{2,3},{3,4},{4,5},{5,6},{6,7},{7,8},{8,9},{9,10},{10,1... | collective-permute-start | bytes 147464 | tf_op jit(solution)/shard_map/ppermute | solution.py:31
  47.3 4.3 %collective-permute-done.7 = f32[4,8,1,4,128]{4,3,2,1,0:T(4,128)S(1)} collective-permute-done((f32[4,8,1,4,128]{4,3,2,1,0:T(4,128)S(1)}, f32[4,8,1,4,128]{4,3,2,1,0:T(4,128)S(1)}, u32[]{:S(2)}, u32[]{:S(2)}) %collective-permute-start.7) | collective-permute-done | bytes 65568 | tf_op jit(solution)/shard_map/ppermute | solution.py:22
  51.6 0.8 select_maximum_fusion.2
  52.5 0.8 multiply_bitcast_fusion.5
  53.4 1.0 fusion.64
  54.3 0.2 fusion.41
  54.6 1.0 fusion.37
  55.6 0.5 fusion.14
  56.1 2.5 %fusion.5 = f32[4,8,4,2,4,128,1]{5,1,6,4,3,2,0:T(8,128)S(1)} fusion(s32[8,128]{1,0:T(8,128)S(1)} %multiply_add_fusion.5, s32[2,4,128]{2,1,0:T(4,128)S(1)} %add_add_fusion, f32[4,8,8,4,128]{4,1,0,3,2:T(8,128)S(1)} %fusion.14), kind=kOutput, calls=%fused_computation.4 | convolution fusion | flops 1611792384 | bytes 1056768 | tf_op jit(solution)/shard_map/dot_general | solution.py:108
  58.6 0.2 copy_add_fusion
  58.8 1.9 %collective-permute-start.10 = (f32[4,8,1,4,128]{4,3,2,1,0:T(4,128)S(1)}, f32[4,8,1,4,128]{4,3,2,1,0:T(4,128)S(1)}, u32[]{:S(2)}, u32[]{:S(2)}) collective-permute-start(f32[4,8,1,4,128]{4,3,2,1,0:T(4,128)S(1)} %get-tuple-element.26), channel_id=1, source_target_pairs={{0,32},{32,64},{64,96},{96,128},{128,160},{160,192},{192,224},{1,3... | collective-permute-start | bytes 196616 | tf_op jit(solution)/shard_map/ppermute | solution.py:22
  60.8 7.0 %collective-permute-start.9 = (f32[4,8,1,4,128]{4,3,2,1,0:T(4,128)S(1)}, f32[4,8,1,4,128]{4,3,2,1,0:T(4,128)S(1)}, u32[]{:S(2)}, u32[]{:S(2)}) collective-permute-start(f32[4,8,1,4,128]{4,3,2,1,0:T(4,128)S(1)} %get-tuple-element.27), channel_id=1, source_target_pairs={{32,0},{64,32},{96,64},{128,96},{160,128},{192,160},{224,192},{33,... | collective-permute-start | bytes 196616 | tf_op jit(solution)/shard_map/ppermute | solution.py:23
  67.8 4.1 %collective-permute-start.8 = (f32[3,8,4,128]{3,2,1,0:T(4,128)S(1)}, f32[3,8,4,128]{3,2,1,0:T(4,128)S(1)}, u32[]{:S(2)}, u32[]{:S(2)}) collective-permute-start(f32[3,8,4,128]{3,2,1,0:T(4,128)S(1)} %slice_bitcast_fusion.12), channel_id=1, source_target_pairs={{0,1},{1,2},{2,3},{3,4},{4,5},{5,6},{6,7},{7,8},{8,9},{9,10},{10,1... | collective-permute-start | bytes 147464 | tf_op jit(solution)/shard_map/ppermute | solution.py:31
  72.0 0.8 select_maximum_fusion
  72.9 0.8 multiply_bitcast_fusion.2
  73.8 1.0 fusion.49
  74.7 0.2 maximum_subtract_fusion.2
  74.9 5.8 %copy.46 = f32[4,8,8,4,128]{1,0,4,3,2:T(4,128)} copy(f32[4,8,8,4,128]{4,3,2,1,0:T(4,128)S(1)} %maximum_subtract_fusion.2) | data formatting | bytes 1048576 | tf_op jit(solution)/shard_map/sub | solution.py:133
  80.8 11.4 %reshape.264 = f32[32,1,4096]{2,1,0:T(1,128)S(1)} reshape(f32[4096,4,8]{2,1,0:T(4,128)} %bitcast.158) | data formatting | bytes 1048576
  92.2 28.2 %all_to_all.18 = f32[32,1,4096]{2,1,0:T(1,128)S(1)} all-to-all(f32[32,1,4096]{2,1,0:T(1,128)S(1)} %reshape.264), channel_id=1, replica_groups=mesh['space'=8,'tm'=32] {'tm'}, dimensions={0} | all-to-all | bytes 1048576 | tf_op jit(solution)/shard_map/all_to_all | solution.py:140
  120.4 0.5 broadcast.416
  120.9 1.9 %reduce.4 = f32[32,4096]{1,0:T(8,128)S(1)} reduce(f32[32,1,4096]{2,1,0:T(1,128)S(1)} %all_to_all.18, f32[]{:T(128)} %broadcast.416), dimensions={1}, to_apply=%all_to_all.13.reduce_sub_computation | reduce | bytes 1048580 | tf_op jit(solution)/shard_map/all_to_all | solution.py:140
  122.8 11.3 %reshape.265 = f32[4096,4,8]{2,1,0:T(4,128)} reshape(f32[32,4096]{1,0:T(8,128)S(1)} %reduce.4) | data formatting | bytes 1048576
  134.1 6.6 %copy.47 = f32[4,32,8,128]{3,2,1,0:T(8,128)S(1)} copy(f32[4,32,8,128]{2,0,3,1:T(4,128)} %bitcast.159) | data formatting | bytes 1048576 | tf_op jit(solution)/shard_map/all_to_all | solution.py:140
  141.3 0.6 multiply_add_fusion.4
  (55 shorter events, 1.4 us)
Async XLA Ops:
  1.5 25.8 %collective-permute-start.2 = (f32[4,8,1,4,128]{4,3,2,1,0:T(4,128)S(1)}, f32[4,8,1,4,128]{4,3,2,1,0:T(4,128)S(1)}, u32[]{:S(2)}, u32[]{:S(2)}) collective-permute-start(f32[4,8,1,4,128]{4,3,2,1,0:T(4,128)S(1)} %get-tuple-element.31), channel_id=1, source_target_pairs={{32,0},{64,32},{96,64},{128,96},{160,128},{192,160},{224,192},{33,... | collective-permute-start | bytes 196616 | tf_op jit(solution)/shard_map/ppermute | solution.py:23
  6.1 21.2 %collective-permute-start.4 = (f32[4,8,1,4,128]{4,3,2,1,0:T(4,128)S(1)}, f32[4,8,1,4,128]{4,3,2,1,0:T(4,128)S(1)}, u32[]{:S(2)}, u32[]{:S(2)}) collective-permute-start(f32[4,8,1,4,128]{4,3,2,1,0:T(4,128)S(1)} %get-tuple-element.30), channel_id=1, source_target_pairs={{0,32},{32,64},{64,96},{96,128},{128,160},{160,192},{192,224},{1,3... | collective-permute-start | bytes 196616 | tf_op jit(solution)/shard_map/ppermute | solution.py:22
  9.5 17.5 %collective-permute-start.1 = (f32[1,4,128]{2,0,1:T(1,128)S(1)}, f32[1,4,128]{2,0,1:T(1,128)S(1)}, u32[]{:S(2)}, u32[]{:S(2)}) collective-permute-start(f32[1,4,128]{2,0,1:T(1,128)S(1)} %get-tuple-element.39), channel_id=1, source_target_pairs={{32,0},{64,32},{96,64},{128,96},{160,128},{192,160},{224,192},{33,... | collective-permute-start | bytes 6152 | tf_op jit(solution)/shard_map/ppermute | solution.py:23
  16.5 10.6 %collective-permute-start.3 = (f32[1,4,128]{2,0,1:T(1,128)S(1)}, f32[1,4,128]{2,0,1:T(1,128)S(1)}, u32[]{:S(2)}, u32[]{:S(2)}) collective-permute-start(f32[1,4,128]{2,0,1:T(1,128)S(1)} %get-tuple-element.38), channel_id=1, source_target_pairs={{0,32},{32,64},{64,96},{96,128},{128,160},{160,192},{192,224},{1,3... | collective-permute-start | bytes 6152 | tf_op jit(solution)/shard_map/ppermute | solution.py:22
  19.2 11.0 %collective-permute-start = (f32[3,8,4,128]{3,2,1,0:T(4,128)S(1)}, f32[3,8,4,128]{3,2,1,0:T(4,128)S(1)}, u32[]{:S(2)}, u32[]{:S(2)}) collective-permute-start(f32[3,8,4,128]{3,2,1,0:T(4,128)S(1)} %slice_bitcast_fusion.14), channel_id=1, source_target_pairs={{0,1},{1,2},{2,3},{3,4},{4,5},{5,6},{6,7},{7,8},{8,9},{9,10},{10,1... | collective-permute-start | bytes 147464 | tf_op jit(solution)/shard_map/ppermute | solution.py:31
  29.2 1.0 copy-start.1
  29.4 1.8 %copy-start.2 = (f32[4,8,8,4,128]{4,3,2,1,0:T(4,128)S(1)}, f32[4,8,8,4,128]{4,3,2,1,0:T(4,128)}, u32[]{:S(2)}) copy-start(f32[4,8,8,4,128]{4,3,2,1,0:T(4,128)} %param.7) | copy-start | bytes 1572868
  35.7 11.6 %collective-permute-start.6 = (f32[4,8,1,4,128]{4,3,2,1,0:T(4,128)S(1)}, f32[4,8,1,4,128]{4,3,2,1,0:T(4,128)S(1)}, u32[]{:S(2)}, u32[]{:S(2)}) collective-permute-start(f32[4,8,1,4,128]{4,3,2,1,0:T(4,128)S(1)} %get-tuple-element.29), channel_id=1, source_target_pairs={{32,0},{64,32},{96,64},{128,96},{160,128},{192,160},{224,192},{33,... | collective-permute-start | bytes 196616 | tf_op jit(solution)/shard_map/ppermute | solution.py:23
  43.0 8.6 %collective-permute-start.7 = (f32[4,8,1,4,128]{4,3,2,1,0:T(4,128)S(1)}, f32[4,8,1,4,128]{4,3,2,1,0:T(4,128)S(1)}, u32[]{:S(2)}, u32[]{:S(2)}) collective-permute-start(f32[4,8,1,4,128]{4,3,2,1,0:T(4,128)S(1)} %get-tuple-element.28), channel_id=1, source_target_pairs={{0,32},{32,64},{64,96},{96,128},{128,160},{160,192},{192,224},{1,3... | collective-permute-start | bytes 196616 | tf_op jit(solution)/shard_map/ppermute | solution.py:22
  44.9 8.4 %collective-permute-start.5 = (f32[3,8,4,128]{3,2,1,0:T(4,128)S(1)}, f32[3,8,4,128]{3,2,1,0:T(4,128)S(1)}, u32[]{:S(2)}, u32[]{:S(2)}) collective-permute-start(f32[3,8,4,128]{3,2,1,0:T(4,128)S(1)} %slice_bitcast_fusion.13), channel_id=1, source_target_pairs={{0,1},{1,2},{2,3},{3,4},{4,5},{5,6},{6,7},{7,8},{8,9},{9,10},{10,1... | collective-permute-start | bytes 147464 | tf_op jit(solution)/shard_map/ppermute | solution.py:31
  58.8 15.0 %copy-start = (f32[4,8,8,4,128]{4,3,2,1,0:T(4,128)}, f32[4,8,8,4,128]{4,3,2,1,0:T(4,128)S(1)}, u32[]{:S(2)}) copy-start(f32[4,8,8,4,128]{4,3,2,1,0:T(4,128)S(1)} %copy_add_fusion) | copy-start | bytes 1572868
  58.8 13.1 %collective-permute-start.10 = (f32[4,8,1,4,128]{4,3,2,1,0:T(4,128)S(1)}, f32[4,8,1,4,128]{4,3,2,1,0:T(4,128)S(1)}, u32[]{:S(2)}, u32[]{:S(2)}) collective-permute-start(f32[4,8,1,4,128]{4,3,2,1,0:T(4,128)S(1)} %get-tuple-element.26), channel_id=1, source_target_pairs={{0,32},{32,64},{64,96},{96,128},{128,160},{160,192},{192,224},{1,3... | collective-permute-start | bytes 196616 | tf_op jit(solution)/shard_map/ppermute | solution.py:22
  60.8 11.2 %collective-permute-start.9 = (f32[4,8,1,4,128]{4,3,2,1,0:T(4,128)S(1)}, f32[4,8,1,4,128]{4,3,2,1,0:T(4,128)S(1)}, u32[]{:S(2)}, u32[]{:S(2)}) collective-permute-start(f32[4,8,1,4,128]{4,3,2,1,0:T(4,128)S(1)} %get-tuple-element.27), channel_id=1, source_target_pairs={{32,0},{64,32},{96,64},{128,96},{160,128},{192,160},{224,192},{33,... | collective-permute-start | bytes 196616 | tf_op jit(solution)/shard_map/ppermute | solution.py:23
  67.8 5.9 %collective-permute-start.8 = (f32[3,8,4,128]{3,2,1,0:T(4,128)S(1)}, f32[3,8,4,128]{3,2,1,0:T(4,128)S(1)}, u32[]{:S(2)}, u32[]{:S(2)}) collective-permute-start(f32[3,8,4,128]{3,2,1,0:T(4,128)S(1)} %slice_bitcast_fusion.12), channel_id=1, source_target_pairs={{0,1},{1,2},{2,3},{3,4},{4,5},{5,6},{6,7},{7,8},{8,9},{9,10},{10,1... | collective-permute-start | bytes 147464 | tf_op jit(solution)/shard_map/ppermute | solution.py:31
where the time goes:
time: 144 us; the launch traced here: 142 us
  starting transfers between devices  44.9 us (31%)
  local copies, waits for them, and re-layouts  41.8 us (29%)
  blocking collectives  28.2 us (20%)
  other arithmetic  13.4 us (9%)
  matrix products  8.03 us (6%)
  waiting for transfers between devices  4.28 us (3%)
    all_to_all x1, blocking collectives, per_device(): lax.all_to_all(flattened, 'tm', split_axis=2, concat_axis=1, tiled=True)  28.2 us
    ppermute x4, starting transfers between devices, extended_2(): after = lax.ppermute(leading, axis, down)  25.8 us
    unnamed x9, local copies, waits for them, and re-layouts  23.5 us
    ppermute x3, starting transfers between devices, passed_along(): return lax.ppermute(shard, axis, pairs)  11.4 us
    ppermute x4, starting transfers between devices, extended_2(): before = lax.ppermute(last, axis, up)  7.68 us
    all_to_all x2, local copies, waits for them, and re-layouts, per_device(): lax.all_to_all(flattened, 'tm', split_axis=2, concat_axis=1, tiled=True)  7.08 us
    sub x1, local copies, waits for them, and re-layouts, residual_of(): return forcing - operate(padded, earlier, visc_pad)  5.83 us
    dot_general x2, matrix products, vanka_patches(): lax.dot_general(scaled, back_table, (((1, 5), (3, 4)), ((), ())), precisi...  5.03 us
  transfers between devices with their start and end apart: 11, of which 1 were waited for; matrix products, arithmetic and copies ran while one was open for 8% of the time, Pallas kernels for 0%

commit v1 on v0

v1 whole, which is shorter than its diff:
```python
import functools

import jax
import jax.numpy as jnp
from jax import lax
from jax.experimental import pallas as pl
from jax.experimental.pallas import tpu as pltpu
from jax.sharding import PartitionSpec as P

MESH = pl.DeviceIdType.MESH
F32 = jnp.float32
BF16 = jnp.bfloat16
DAMPING = 0.8
STABILIZE = 0.1


def iota(shape, dim):
    return lax.broadcasted_iota(jnp.int32, shape, dim)


def cell_index(q):
    return (q // 8) * 8 + (q // 4 % 2) * 4 + (q % 2) * 2


def build_bank(bank_ref, lhs_ref):
    j = iota((32, 64), 0)
    q = iota((32, 64), 1)
    spread = (j == cell_index(q % 32) + q // 32).astype(BF16)
    p = iota((64, 32), 0)
    i = iota((64, 32), 1)
    gather = (i == cell_index(p % 32) + p // 32).astype(BF16)
    same = (iota((64, 64), 0) // 2 % 2) == (iota((64, 64), 1) // 2 % 2)
    wide = jnp.dot(bank_ref[...].reshape(128, 32), spread, preferred_element_type=F32).astype(BF16)
    parts = []
    for kind in range(4):
        part = jnp.dot(gather, wide[32 * kind : 32 * kind + 32], preferred_element_type=F32)
        parts.append(jnp.where(same, part, 0.0).astype(BF16))
    lhs_ref[...] = jnp.concatenate(parts, axis=1)


def build_kinds(kind_ref, mask_ref):
    upper = iota((8, 64), 0) // 2 % 2 == 0
    double = (iota((64, 128), 0) == iota((64, 128), 1) // 2).astype(BF16)
    for g in range(4):
        pair = kind_ref[g].astype(F32)
        rows = jnp.where(upper, pair[0:1], pair[1:2]).astype(BF16)
        kinds = jnp.dot(rows, double, preferred_element_type=F32)
        for kind in range(4):
            mask = (kinds == float(kind)).astype(F32)
            mask_ref[g, kind] = jnp.concatenate([mask, mask], axis=0).astype(BF16)


def shift_x(values, left, right):
    first = jnp.concatenate([left, values[0, 0:4]], axis=0)
    last = jnp.concatenate([values[3, 4:8], right], axis=0)
    low = iota((3, 8, 128), 1) < 4
    inner = pltpu.roll(jnp.where(low, values[1:4], values[0:3]), 4, 1)
    return (
        jnp.concatenate([first[None], inner], axis=0),
        jnp.concatenate([inner, last[None]], axis=0),
    )


def shifts_yz(values):
    return (
        pltpu.roll(values, 1, 1),
        pltpu.roll(values, 7, 1),
        pltpu.roll(values, 1, 2),
        pltpu.roll(values, 127, 2),
    )


def edge_masks():
    y = iota((4, 8, 128), 1) % 4
    z = iota((4, 8, 128), 2)
    return y != 0, y != 3, z != 0, z != 127


def build_coefficients(viscosity, left, right, coef_ref):
    xm, xp = shift_x(viscosity, left, right)
    ym, yp, zm, zp = shifts_yz(viscosity)
    total = jnp.ones_like(viscosity)
    for n, (near, mask) in enumerate(zip((xm, xp, ym, yp, zm, zp), (None, None) + edge_masks())):
        if mask is not None:
            near = jnp.where(mask, near, 0.0)
        kappa = 0.5 * (viscosity + near)
        total = total + kappa
        if mask is not None:
            kappa = jnp.where(mask, kappa, 0.0)
        coef_ref[1 + n] = kappa
    coef_ref[0] = total


def residual(t, cur, left, right, forcing, coef_ref):
    mym, myp, mzm, mzp = edge_masks()
    pressure = cur[3, t + 1]
    pxm, pxp = shift_x(pressure, left[3, t], right[3, t])
    pym, pyp, pzm, pzp = shifts_yz(pressure)
    pym = jnp.where(mym, pym, 0.0)
    pyp = jnp.where(myp, pyp, 0.0)
    pzm = jnp.where(mzm, pzm, 0.0)
    pzp = jnp.where(mzp, pzp, 0.0)
    gradients = (pxp - pxm, pyp - pym, pzp - pzm)
    out = []
    divergence = None
    for c in range(3):
        value = cur[c, t + 1]
        xm, xp = shift_x(value, left[c, t], right[c, t])
        ym, yp, zm, zp = shifts_yz(value)
        flow = coef_ref[1] * xm + coef_ref[2] * xp
        flow = flow + (coef_ref[3] * ym + coef_ref[4] * yp)
        flow = flow + (coef_ref[5] * zm + coef_ref[6] * zp)
        out.append(
            forcing[c, t] + cur[c, t] - coef_ref[0] * value + flow - 0.5 * gradients[c]
        )
        if c == 0:
            divergence = xp - xm
        elif c == 1:
            divergence = divergence + (jnp.where(myp, yp, 0.0) - jnp.where(mym, ym, 0.0))
        else:
            divergence = divergence + (jnp.where(mzp, zp, 0.0) - jnp.where(mzm, zm, 0.0))
    around = (pxm + pxp) + (pym + pyp) + (pzm + pzp)
    out.append(
        forcing[3, t] - STABILIZE * (6.0 * pressure - around) + 0.5 * divergence
    )
    return out


def smooth(t, cur, left, right, forcing, coef_ref, lhs_ref, mask_ref, nxt, send_left, send_right):
    resid = residual(t, cur, left, right, forcing, coef_ref)
    even = iota((4, 8, 128), 2) % 2 == 0
    evens = []
    odds = []
    for value in resid:
        evens.append(jnp.where(even, value, pltpu.roll(value, 1, 2)))
        odds.append(jnp.where(even, pltpu.roll(value, 127, 2), value))
    columns = []
    for g in range(4):
        stack = jnp.concatenate([v[g] for v in evens] + [v[g] for v in odds], axis=0)
        stack = stack.astype(BF16).reshape(4, 16, 128)
        masked = [(stack * mask_ref[g, kind]).reshape(64, 128) for kind in range(4)]
        columns.append(jnp.concatenate(masked, axis=0))
    product = jnp.dot(
        lhs_ref[...], jnp.concatenate(columns, axis=1), preferred_element_type=F32
    )
    even = even[0]
    for g in range(4):
        for c in range(4):
            part = product[8 * c : 8 * c + 8, 128 * g : 128 * g + 128]
            other = product[32 + 8 * c : 40 + 8 * c, 128 * g : 128 * g + 128]
            value = cur[c, t + 1, g] + DAMPING * jnp.where(even, part, other)
            nxt[c, t + 1, g] = value
            if g == 0:
                send_left[c, t] = value[0:4]
            if g == 3:
                send_right[c, t] = value[4:8]


def kernel(
    init5, init, forc, table, vclass, bank, kind,
    smoothed, coarse,
    buf0, buf1, buf2, forcing, lefts, rights, outl, outr, vout, vin, coef, lhs, mask, acc, parts, recv,
    load_sem, send_sem, recv_sem, vsend_sem, vrecv_sem, psend_sem, precv_sem,
):
    sx = lax.axis_index("space")
    tb = lax.axis_index("tm")
    bufs = (buf0, buf1, buf2)
    has_left, has_right = sx > 0, sx < 7
    has_before, has_after = tb > 0, tb < 31

    barrier = pltpu.get_barrier_semaphore()

    def greet(step, carry):
        peer = lax.rem(tb + step, 32)
        pl.semaphore_signal(barrier, inc=1, device_id={"tm": peer}, device_id_type=MESH)
        return carry

    lax.fori_loop(1, 32, greet, 0)

    @pl.when(has_left)
    def _():
        pl.semaphore_signal(barrier, inc=1, device_id={"space": sx - 1}, device_id_type=MESH)

    @pl.when(has_right)
    def _():
        pl.semaphore_signal(barrier, inc=1, device_id={"space": sx + 1}, device_id_type=MESH)

    load_a = pltpu.make_async_copy(init, buf0.at[:, 1:9], load_sem.at[0])
    load_b = pltpu.make_async_copy(forc, forcing, load_sem.at[1])
    load_a.start()
    load_b.start()

    pl.semaphore_wait(barrier, 31 + has_left.astype(jnp.int32) + has_right.astype(jnp.int32))

    def exchange(s):
        if s == 0:
            from_left, from_right, last = init5.at[:, :, 0], init5.at[:, :, 7], init.at[0:3, 7]
        else:
            from_left, from_right, last = outl.at[s - 1], outr.at[s - 1], bufs[s].at[0:3, 8]
        to_left = pltpu.make_async_remote_copy(
            from_left, rights.at[s], send_sem.at[s, 0], recv_sem.at[s, 1],
            device_id={"space": sx - 1}, device_id_type=MESH,
        )
        to_right = pltpu.make_async_remote_copy(
            from_right, lefts.at[s], send_sem.at[s, 1], recv_sem.at[s, 0],
            device_id={"space": sx + 1}, device_id_type=MESH,
        )
        to_after = pltpu.make_async_remote_copy(
            last, bufs[s].at[0:3, 0], send_sem.at[s, 2], recv_sem.at[s, 2],
            device_id={"tm": tb + 1}, device_id_type=MESH,
        )
        return to_left, to_right, to_after

    def start(s):
        to_left, to_right, to_after = exchange(s)
        pl.when(has_left)(to_left.start)
        pl.when(has_right)(to_right.start)
        pl.when(has_after)(to_after.start)

    def arrive(s):
        to_left, to_right, to_after = exchange(s)
        pl.when(has_left)(to_right.wait_recv)
        pl.when(has_right)(to_left.wait_recv)
        pl.when(has_before)(to_after.wait_recv)

    def sent(s):
        to_left, to_right, to_after = exchange(s)
        pl.when(has_left)(to_left.wait_send)
        pl.when(has_right)(to_right.wait_send)
        pl.when(has_after)(to_after.wait_send)

    start(0)

    viscosity = jnp.zeros((4, 8, 128), F32)
    for label in range(8):
        viscosity = jnp.where(vclass[...] == label, table[label], viscosity)
    vout[0] = viscosity[0, 0:4]
    vout[1] = viscosity[3, 4:8]
    v_left = pltpu.make_async_remote_copy(
        vout.at[0], vin.at[1], vsend_sem.at[0], vrecv_sem.at[1],
        device_id={"space": sx - 1}, device_id_type=MESH,
    )
    v_right = pltpu.make_async_remote_copy(
        vout.at[1], vin.at[0], vsend_sem.at[1], vrecv_sem.at[0],
        device_id={"space": sx + 1}, device_id_type=MESH,
    )
    pl.when(has_left)(v_left.start)
    pl.when(has_right)(v_right.start)

    @pl.when(sx == 0)
    def _():
        vin[0] = jnp.zeros((4, 128), F32)
        for s in range(3):
            lefts[s] = jnp.zeros((4, 8, 4, 128), F32)

    @pl.when(sx == 7)
    def _():
        vin[1] = jnp.zeros((4, 128), F32)
        for s in range(3):
            rights[s] = jnp.zeros((4, 8, 4, 128), F32)

    @pl.when(tb == 0)
    def _():
        for buf in bufs:
            buf[0:3, 0] = jnp.zeros((3, 4, 8, 128), F32)

    build_bank(bank, lhs)
    build_kinds(kind, mask)
    acc[...] = jnp.zeros_like(acc)

    pl.when(has_left)(v_right.wait_recv)
    pl.when(has_right)(v_left.wait_recv)
    build_coefficients(viscosity, vin[0], vin[1], coef)
    load_a.wait()
    load_b.wait()

    for s in range(2):
        arrive(s)

        def sweep(t, carry, s=s):
            smooth(
                t, bufs[s], lefts.at[s], rights.at[s], forcing, coef, lhs, mask,
                bufs[s + 1], outl.at[s], outr.at[s],
            )
            return carry

        lax.fori_loop(0, 8, sweep, 0)
        start(s + 1)

    store = pltpu.make_async_copy(buf2.at[:, 1:9], smoothed, load_sem.at[2])
    store.start()
    arrive(2)

    def finish(t, carry):
        resid = residual(t, buf2, lefts.at[2], rights.at[2], forcing, coef)
        j = lax.rem(tb, 4) * 8 + t
        near = (32 - j).astype(F32) * (1.0 / 1024.0)
        far = j.astype(F32) * (1.0 / 1024.0)
        for c in range(4):
            acc[0, c] += near * resid[c]
            acc[1, c] += far * resid[c]
        return carry

    lax.fori_loop(0, 8, finish, 0)
    for half in range(2):
        for c in range(4):
            for g in range(4):
                parts[pl.ds(64 * g + 4 * half + c, 8, stride=8), :] = acc[half, c, g]

    def piece(step):
        peer = lax.rem(tb + step, 32)
        return pltpu.make_async_remote_copy(
            parts.at[pl.ds(pl.multiple_of(peer * 8, 8), 8)], recv.at[tb], psend_sem.at[step], precv_sem.at[tb],
            device_id={"tm": peer}, device_id_type=MESH,
        )

    def send(step, carry):
        piece(step).start()
        return carry

    lax.fori_loop(1, 32, send, 0)
    recv[tb] = parts[pl.ds(pl.multiple_of(tb * 8, 8), 8), :]

    def take(step, carry):
        source = lax.rem(tb + step, 32)
        pltpu.make_async_remote_copy(
            parts.at[0:8], recv.at[source], psend_sem.at[step], precv_sem.at[source],
            device_id={"tm": source}, device_id_type=MESH,
        ).wait_recv()
        return carry

    lax.fori_loop(1, 32, take, 0)
    before = jnp.zeros((4, 128), F32)
    for k in range(8):
        block = (recv[4 * k] + recv[4 * k + 1]) + (recv[4 * k + 2] + recv[4 * k + 3])
        level = block[0:4] + before
        before = block[4:8]
        for c in range(4):
            coarse[c, k : k + 1, :] = level[c : c + 1]

    def drain(step, carry):
        piece(step).wait_send()
        return carry

    lax.fori_loop(1, 32, drain, 0)
    for s in range(3):
        sent(s)
    pl.when(has_left)(v_left.wait_send)
    pl.when(has_right)(v_right.wait_send)
    store.wait()


def per_device(initial_guess, forcing, visc_table, visc_class, inverse_bank, patch_kind):
    hbm = pl.BlockSpec(memory_space=pl.ANY)
    vmem = pl.BlockSpec(memory_space=pltpu.VMEM)
    smem = pl.BlockSpec(memory_space=pltpu.SMEM)
    dma = pltpu.SemaphoreType.DMA
    smoothed, coarse = pl.pallas_call(
        kernel,
        out_shape=(
            jax.ShapeDtypeStruct((4, 8, 4, 8, 128), F32),
            jax.ShapeDtypeStruct((4, 8, 128), F32),
        ),
        in_specs=[hbm, hbm, hbm, smem, vmem, vmem, vmem],
        out_specs=(hbm, vmem),
        scratch_shapes=[
            pltpu.VMEM((4, 9, 4, 8, 128), F32),
            pltpu.VMEM((4, 9, 4, 8, 128), F32),
            pltpu.VMEM((4, 9, 4, 8, 128), F32),
            pltpu.VMEM((4, 8, 4, 8, 128), F32),
            pltpu.VMEM((3, 4, 8, 4, 128), F32),
            pltpu.VMEM((3, 4, 8, 4, 128), F32),
            pltpu.VMEM((2, 4, 8, 4, 128), F32),
            pltpu.VMEM((2, 4, 8, 4, 128), F32),
            pltpu.VMEM((2, 4, 128), F32),
            pltpu.VMEM((2, 4, 128), F32),
            pltpu.VMEM((7, 4, 8, 128), F32),
            pltpu.VMEM((64, 256), BF16),
            pltpu.VMEM((4, 4, 16, 128), BF16),
            pltpu.VMEM((2, 4, 4, 8, 128), F32),
            pltpu.VMEM((256, 128), F32),
            pltpu.VMEM((32, 8, 128), F32),
            dma((3,)),
            dma((3, 3)),
            dma((3, 3)),
            dma((2,)),
            dma((2,)),
            dma((32,)),
            dma((32,)),
        ],
        compiler_params=pltpu.CompilerParams(
            collective_id=0, has_side_effects=True, vmem_limit_bytes=24 * 1024 * 1024
        ),
    )(
        initial_guess,
        initial_guess.reshape(4, 8, 4, 8, 128),
        forcing.reshape(4, 8, 4, 8, 128),
        visc_table,
        visc_class.reshape(4, 8, 128),
        inverse_bank,
        patch_kind,
    )
    return smoothed.reshape(4, 8, 8, 4, 128), coarse


def solution(mesh):
    return jax.shard_map(
        per_device,
        mesh=mesh,
        in_specs=(
            P(None, "tm", "space", None, None),
            P(None, "tm", "space", None, None),
            P(),
            P("space", None, None),
            P(),
            P("space", None, None),
        ),
        out_specs=(P(None, "tm", "space", None, None), P(None, None, ("space", "tm"))),
        check_vma=False,
    )
```

time: 144 us -> 44 us (0.31); the launches traced: 142 us -> 43.5 us
  starting transfers between devices: 44.9 us -> 0 us
  Pallas kernels: 0 us -> 37.2 us
  local copies, waits for them, and re-layouts: 41.8 us -> 5.63 us
  blocking collectives: 28.2 us -> 0 us
  other arithmetic: 13.4 us -> 0 us
  matrix products: 8.03 us -> 0 us
  waiting for transfers between devices: 4.28 us -> 0 us
    ppermute x11 -> x0, starting transfers between devices: 44.9 us -> none  [the longest x4 25.8 us: extended_2(): after = lax.ppermute(leading, axis, down)]
    pallas_call x0 -> x1, Pallas kernels: none -> 37.2 us  [per_device(): pl.pallas_call(kernel, out_shape=(jax.ShapeDtypeStruct((4, 8, 4, 8, 128),...]
    all_to_all x1 -> x0, blocking collectives: 28.2 us -> none  [per_device(): lax.all_to_all(flattened, 'tm', split_axis=2, concat_axis=1, tiled=True)]
    unnamed x9 -> x14, local copies, waits for them, and re-layouts: 23.5 us -> 5.63 us
    dot_general x6 -> x0, matrix products: 8.03 us -> none  [the longest x2 5.03 us: vanka_patches(): lax.dot_general(scaled, back_table, (((1, 5), (3, 4)), ((), ())), precisi...]
    all_to_all x2 -> x0, local copies, waits for them, and re-layouts: 7.08 us -> none  [per_device(): lax.all_to_all(flattened, 'tm', split_axis=2, concat_axis=1, tiled=True)]
    sub x1 -> x0, local copies, waits for them, and re-layouts: 5.83 us -> none  [residual_of(): return forcing - operate(padded, earlier, visc_pad)]
    ppermute x11 -> x0, waiting for transfers between devices: 4.28 us -> none  [the longest x4 4.26 us: extended_2(): before = lax.ppermute(last, axis, up)]
  transfers between devices with their start and end apart: 11 -> 0, of which waited for: 1 -> 0; matrix products, arithmetic and copies ran while one was open for 8% -> 0% of each run, Pallas kernels for 0% -> 0%
where the time goes in v1:
time: 44 us; the launch traced here: 43.5 us
  Pallas kernels  37.2 us (85%)
  local copies, waits for them, and re-layouts  5.63 us (13%)
  between operations  0.66 us (2%)
    pallas_call x1, Pallas kernels, per_device(): pl.pallas_call(kernel, out_shape=(jax.ShapeDtypeStruct((4, 8, 4, 8, 128),...  37.2 us
    unnamed x14, local copies, waits for them, and re-layouts  5.63 us

profile of v1, /device:TPU:5, one launch (start us, length us, event | category | flops | bytes accessed | tf_op | source)
XLA Modules:
  0.0 43.5 jit_solution(12295628620236287138)
XLA Ops:
  0.6 0.0 copy-start.4
  0.6 0.0 copy-start.5
  0.7 0.7 %copy-done.4 = s32[4,2,64]{2,1,0:T(2,128)S(1)} copy-done((s32[4,2,64]{2,1,0:T(2,128)S(1)}, s32[4,2,64]{2,1,0:T(2,128)}, u32[]{:S(2)}) %copy-start.4) | copy-done | bytes 2072
  1.3 0.0 copy-done.5
  1.3 0.0 copy-start
  1.3 1.0 %copy-done = f32[4,8,8,4,128]{4,3,2,1,0:T(4,128)S(1)} copy-done((f32[4,8,8,4,128]{4,3,2,1,0:T(4,128)S(1)}, f32[4,8,8,4,128]{4,3,2,1,0:T(4,128)}, u32[]{:S(2)}) %copy-start) | copy-done | bytes 524312
  2.4 0.0 copy-start.1
  2.4 1.0 %copy-done.1 = f32[4,8,8,4,128]{4,3,2,1,0:T(4,128)S(1)} copy-done((f32[4,8,8,4,128]{4,3,2,1,0:T(4,128)S(1)}, f32[4,8,8,4,128]{4,3,2,1,0:T(4,128)}, u32[]{:S(2)}) %copy-start.1) | copy-done | bytes 524312
  3.4 0.0 copy-start.2
  3.4 0.8 %copy-done.2 = bf16[4,32,32]{2,1,0:T(8,128)(2,1)S(1)} copy-done((bf16[4,32,32]{2,1,0:T(8,128)(2,1)S(1)}, bf16[4,32,32]{2,1,0:T(8,128)(2,1)}, u32[]{:S(2)}) %copy-start.2) | copy-done | bytes 8216
  4.2 0.0 copy-start.3
  4.2 0.7 %copy-done.3 = s32[8,4,128]{2,1,0:T(4,128)S(1)} copy-done((s32[8,4,128]{2,1,0:T(4,128)S(1)}, s32[8,4,128]{2,1,0:T(4,128)}, u32[]{:S(2)}) %copy-start.3) | copy-done | bytes 16408
  4.9 37.2 %shard_map.77 = (f32[4,8,4,8,128]{4,3,2,1,0:T(8,128)S(1)}, f32[4,8,128]{2,1,0:T(8,128)S(1)}) custom-call(f32[4,8,8,4,128]{4,3,2,1,0:T(4,128)S(1)} %copy-done, f32[4,8,4,8,128]{4,3,2,1,0:T(8,128)S(1)} %bitcast.4, f32[4,8,4,8,128]{4,3,2,1,0:T(8,128)S(1)} %bitcast.5, f32[8]{0:T(128)S(1)} %copy-done.5, s32[4,8,128]{2,1,0:T(8,128)S(1)} %bitcast.7, ...), custom_call_target="tpu_custom_call" | custom-call | tf_op jit(solution)/shard_map/pallas_call | solution.py:358
  42.1 0.8 %copy.10 = f32[4,8,8,4,128]{4,3,2,1,0:T(4,128)} copy(f32[4,8,8,4,128]{4,3,2,1,0:T(4,128)S(1)} %bitcast.6) | data formatting | bytes 1048576
  42.9 0.6 %copy.11 = f32[4,8,128]{2,1,0:T(8,128)} copy(f32[4,8,128]{2,1,0:T(8,128)S(1)} %get-tuple-element.9) | data formatting | bytes 32768
Async XLA Ops:
  0.6 0.7 %copy-start.4 = (s32[4,2,64]{2,1,0:T(2,128)S(1)}, s32[4,2,64]{2,1,0:T(2,128)}, u32[]{:S(2)}) copy-start(s32[4,2,64]{2,1,0:T(2,128)} %kind.1) | copy-start | bytes 6148
  0.6 0.7 %copy-start.5 = (f32[8]{0:T(128)S(1)}, f32[8]{0:T(128)}, u32[]{:S(2)}) copy-start(f32[8]{0:T(128)} %table.1) | copy-start | bytes 100
  1.3 1.0 %copy-start = (f32[4,8,8,4,128]{4,3,2,1,0:T(4,128)S(1)}, f32[4,8,8,4,128]{4,3,2,1,0:T(4,128)}, u32[]{:S(2)}) copy-start(f32[4,8,8,4,128]{4,3,2,1,0:T(4,128)} %init5.1) | copy-start | bytes 1572868
  2.4 1.0 %copy-start.1 = (f32[4,8,8,4,128]{4,3,2,1,0:T(4,128)S(1)}, f32[4,8,8,4,128]{4,3,2,1,0:T(4,128)}, u32[]{:S(2)}) copy-start(f32[4,8,8,4,128]{4,3,2,1,0:T(4,128)} %param.7) | copy-start | bytes 1572868
  3.4 0.8 %copy-start.2 = (bf16[4,32,32]{2,1,0:T(8,128)(2,1)S(1)}, bf16[4,32,32]{2,1,0:T(8,128)(2,1)}, u32[]{:S(2)}) copy-start(bf16[4,32,32]{2,1,0:T(8,128)(2,1)} %bank.1) | copy-start | bytes 24580
  4.2 0.7 %copy-start.3 = (s32[8,4,128]{2,1,0:T(4,128)S(1)}, s32[8,4,128]{2,1,0:T(4,128)}, u32[]{:S(2)}) copy-start(s32[8,4,128]{2,1,0:T(4,128)} %param.9) | copy-start | bytes 49156

commit v2 on v1

v2 whole, which is shorter than its diff:
```python
import functools

import jax
import jax.numpy as jnp
from jax import lax
from jax.experimental import pallas as pl
from jax.experimental.pallas import tpu as pltpu
from jax.sharding import PartitionSpec as P

MESH = pl.DeviceIdType.MESH
F32 = jnp.float32
BF16 = jnp.bfloat16
DAMPING = 0.8
STABILIZE = 0.1


def iota(shape, dim):
    return lax.broadcasted_iota(jnp.int32, shape, dim)


def cell_index(q):
    return (q // 8) * 8 + (q // 4 % 2) * 4 + (q % 2) * 2


def build_bank(bank_ref, lhs_ref):
    j = iota((32, 64), 0)
    q = iota((32, 64), 1)
    spread = (j == cell_index(q % 32) + q // 32).astype(BF16)
    p = iota((64, 32), 0)
    i = iota((64, 32), 1)
    gather = (i == cell_index(p % 32) + p // 32).astype(BF16)
    same = (iota((64, 64), 0) // 2 % 2) == (iota((64, 64), 1) // 2 % 2)
    wide = jnp.dot(bank_ref[...].reshape(128, 32), spread, preferred_element_type=F32).astype(BF16)
    parts = []
    for kind in range(4):
        part = jnp.dot(gather, wide[32 * kind : 32 * kind + 32], preferred_element_type=F32)
        parts.append(jnp.where(same, part, 0.0).astype(BF16))
    lhs_ref[...] = jnp.concatenate(parts, axis=1)


def build_kinds(kind_ref, mask_ref):
    upper = iota((8, 64), 0) // 2 % 2 == 0
    double = (iota((64, 128), 0) == iota((64, 128), 1) // 2).astype(BF16)
    for g in range(4):
        pair = kind_ref[g].astype(F32)
        rows = jnp.where(upper, pair[0:1], pair[1:2]).astype(BF16)
        kinds = jnp.dot(rows, double, preferred_element_type=F32)
        for kind in range(4):
            mask = (kinds == float(kind)).astype(F32)
            mask_ref[g, kind] = jnp.concatenate([mask, mask], axis=0).astype(BF16)


def shift_x(values, left, right):
    first = jnp.concatenate([left, values[0, 0:4]], axis=0)
    last = jnp.concatenate([values[3, 4:8], right], axis=0)
    low = iota((3, 8, 128), 1) < 4
    inner = pltpu.roll(jnp.where(low, values[1:4], values[0:3]), 4, 1)
    return (
        jnp.concatenate([first[None], inner], axis=0),
        jnp.concatenate([inner, last[None]], axis=0),
    )


def shifts_yz(values):
    return (
        pltpu.roll(values, 1, 1),
        pltpu.roll(values, 7, 1),
        pltpu.roll(values, 1, 2),
        pltpu.roll(values, 127, 2),
    )


def edge_masks():
    y = iota((4, 8, 128), 1) % 4
    z = iota((4, 8, 128), 2)
    return y != 0, y != 3, z != 0, z != 127


def build_coefficients(viscosity, left, right, coef_ref):
    xm, xp = shift_x(viscosity, left, right)
    ym, yp, zm, zp = shifts_yz(viscosity)
    total = jnp.zeros_like(viscosity)
    for n, (near, mask) in enumerate(zip((xm, xp, ym, yp, zm, zp), (None, None) + edge_masks())):
        if mask is not None:
            near = jnp.where(mask, near, 0.0)
        kappa = 0.5 * (viscosity + near)
        total = total + kappa
        if mask is not None:
            kappa = jnp.where(mask, kappa, 0.0)
        coef_ref[1 + n] = kappa
    coef_ref[0] = total + 1.0
    coef_ref[7] = total


def residual(now, left, right, base, diagonal, coef_ref):
    mym, myp, mzm, mzp = edge_masks()
    pressure = now[3]
    pxm, pxp = shift_x(pressure, left[3], right[3])
    pym, pyp, pzm, pzp = shifts_yz(pressure)
    pym = jnp.where(mym, pym, 0.0)
    pyp = jnp.where(myp, pyp, 0.0)
    pzm = jnp.where(mzm, pzm, 0.0)
    pzp = jnp.where(mzp, pzp, 0.0)
    gradients = (pxp - pxm, pyp - pym, pzp - pzm)
    out = []
    divergence = None
    for c in range(3):
        value = now[c]
        xm, xp = shift_x(value, left[c], right[c])
        ym, yp, zm, zp = shifts_yz(value)
        flow = coef_ref[1] * xm + coef_ref[2] * xp
        flow = flow + (coef_ref[3] * ym + coef_ref[4] * yp)
        flow = flow + (coef_ref[5] * zm + coef_ref[6] * zp)
        out.append(base[c] - diagonal * value + flow - 0.5 * gradients[c])
        if c == 0:
            divergence = xp - xm
        elif c == 1:
            divergence = divergence + (jnp.where(myp, yp, 0.0) - jnp.where(mym, ym, 0.0))
        else:
            divergence = divergence + (jnp.where(mzp, zp, 0.0) - jnp.where(mzm, zm, 0.0))
    around = (pxm + pxp) + (pym + pyp) + (pzm + pzp)
    out.append(base[3] - STABILIZE * (6.0 * pressure - around) + 0.5 * divergence)
    return out


def corrections(resid, lhs_ref, mask_ref):
    even = iota((4, 8, 128), 2) % 2 == 0
    evens = []
    odds = []
    for value in resid:
        evens.append(jnp.where(even, value, pltpu.roll(value, 1, 2)))
        odds.append(jnp.where(even, pltpu.roll(value, 127, 2), value))
    columns = []
    for g in range(4):
        stack = jnp.concatenate([v[g] for v in evens] + [v[g] for v in odds], axis=0)
        stack = stack.astype(BF16).reshape(4, 16, 128)
        masked = [(stack * mask_ref[g, kind]).reshape(64, 128) for kind in range(4)]
        columns.append(jnp.concatenate(masked, axis=0))
    product = jnp.dot(
        lhs_ref[...], jnp.concatenate(columns, axis=1), preferred_element_type=F32
    )
    even = even[0]
    out = []
    for g in range(4):
        across = slice(128 * g, 128 * g + 128)
        out.append(
            [
                DAMPING
                * jnp.where(even, product[8 * c : 8 * c + 8, across], product[32 + 8 * c : 40 + 8 * c, across])
                for c in range(4)
            ]
        )
    return out


def time_sums(load):
    plain = load(0)
    ramp = None
    for t in range(1, 8):
        value = load(t)
        plain = plain + value
        ramp = value * float(t) if ramp is None else ramp + value * float(t)
    return plain, ramp


def kernel(
    init5, init, forc, table_in, vclass_in, bank_in, kind_in,
    smoothed, coarse, table, vclass, bank, kind,
    buf0, buf1, forcing, lefts, rights, outl, outr, vout, vin, coef, lhs, mask,
    weighted, weighted_f, gout, gin, parts, edge, recv,
    load_sem, send_sem, recv_sem, tsend_sem, trecv_sem, vsend_sem, vrecv_sem, gsend_sem, grecv_sem, psend_sem, precv_sem,
):
    sx = lax.axis_index("space")
    tb = lax.axis_index("tm")
    has_left, has_right = sx > 0, sx < 7
    has_before, has_after = tb > 0, tb < 31
    to_left, to_right, to_after = {"space": sx - 1}, {"space": sx + 1}, {"tm": tb + 1}

    barrier = pltpu.get_barrier_semaphore()

    @pl.when(has_left)
    def _():
        pl.semaphore_signal(barrier, inc=1, device_id=to_left, device_id_type=MESH)

    @pl.when(has_right)
    def _():
        pl.semaphore_signal(barrier, inc=1, device_id=to_right, device_id_type=MESH)

    def greet(step, carry):
        peer = lax.rem(tb + step, 32)
        pl.semaphore_signal(barrier, inc=1, device_id={"tm": peer}, device_id_type=MESH)
        return carry

    lax.fori_loop(1, 32, greet, 0)

    loads = [
        pltpu.make_async_copy(table_in, table, load_sem.at[0]),
        pltpu.make_async_copy(vclass_in, vclass, load_sem.at[1]),
        pltpu.make_async_copy(bank_in, bank, load_sem.at[2]),
        pltpu.make_async_copy(kind_in, kind, load_sem.at[3]),
        pltpu.make_async_copy(init, buf0.at[:, 1:9], load_sem.at[4]),
        pltpu.make_async_copy(forc, forcing, load_sem.at[5]),
    ]
    for copy in loads:
        copy.start()

    pl.semaphore_wait(barrier, 31 + has_left.astype(jnp.int32) + has_right.astype(jnp.int32))

    def remote(source, target, send, receive, device):
        return pltpu.make_async_remote_copy(
            source, target, send, receive, device_id=device, device_id_type=MESH
        )

    def chunk_copies(s, i):
        if s == 0:
            steps = pl.ds(6 - 2 * i, 2)
            from_left, from_right = init5.at[:, steps, 0], init5.at[:, steps, 7]
        else:
            from_left, from_right = outl.at[i], outr.at[i]
        return (
            remote(from_left, rights.at[s, i], send_sem.at[0], recv_sem.at[s, 1, i], to_left),
            remote(from_right, lefts.at[s, i], send_sem.at[1], recv_sem.at[s, 0, i], to_right),
        )

    def start_chunk(s, i):
        leftward, rightward = chunk_copies(s, i)
        pl.when(has_left)(leftward.start)
        pl.when(has_right)(rightward.start)

    def arrive_chunk(s, i):
        leftward, rightward = chunk_copies(s, i)
        pl.when(has_left)(rightward.wait_recv)
        pl.when(has_right)(leftward.wait_recv)

    later = [
        remote(init.at[0:3, 7], buf0.at[0:3, 0], tsend_sem.at[0], trecv_sem.at[0], to_after),
        remote(buf1.at[0:3, 8], buf1.at[0:3, 0], tsend_sem.at[1], trecv_sem.at[1], to_after),
    ]

    start_chunk(0, 0)
    start_chunk(0, 1)
    pl.when(has_after)(later[0].start)
    start_chunk(0, 2)
    start_chunk(0, 3)

    loads[0].wait()
    loads[1].wait()
    viscosity = jnp.zeros((4, 8, 128), F32)
    for label in range(8):
        viscosity = jnp.where(vclass[...] == label, table[label], viscosity)
    vout[0] = viscosity[0, 0:4]
    vout[1] = viscosity[3, 4:8]
    v_left = remote(vout.at[0], vin.at[1], vsend_sem.at[0], vrecv_sem.at[1], to_left)
    v_right = remote(vout.at[1], vin.at[0], vsend_sem.at[1], vrecv_sem.at[0], to_right)
    pl.when(has_left)(v_left.start)
    pl.when(has_right)(v_right.start)

    @pl.when(sx == 0)
    def _():
        vin[0] = jnp.zeros((4, 128), F32)
        lefts[...] = jnp.zeros_like(lefts)

    @pl.when(sx == 7)
    def _():
        vin[1] = jnp.zeros((4, 128), F32)
        rights[...] = jnp.zeros_like(rights)

    @pl.when(tb == 0)
    def _():
        for buf in (buf0, buf1):
            buf[0:3, 0] = jnp.zeros((3, 4, 8, 128), F32)

    loads[2].wait()
    build_bank(bank, lhs)
    loads[3].wait()
    build_kinds(kind, mask)

    first = (lax.rem(tb, 4) * 8).astype(F32) * (1.0 / 1024.0)

    def weigh(plain, ramp):
        far = first * plain + ramp * (1.0 / 1024.0)
        return plain * (1.0 / 32.0) - far, far

    loads[5].wait()
    for c in range(4):
        near, far = weigh(*time_sums(lambda t, c=c: forcing[c, t]))
        weighted_f[0, c] = near
        weighted_f[1, c] = far

    pl.when(has_left)(v_right.wait_recv)
    pl.when(has_right)(v_left.wait_recv)
    build_coefficients(viscosity, vin[0], vin[1], coef)
    loads[4].wait()

    for s in range(2):
        cur = (buf0, buf1)[s]

        def sweep(i, carry, s=s, cur=cur):
            arrive_chunk(s, i)

            @pl.when(jnp.logical_and(i == 3, has_before))
            def _():
                later[s].wait_recv()

            for part in range(2):
                t = 6 - 2 * i + part
                now = [cur[c, t + 1] for c in range(4)]
                base = [forcing[c, t] + cur[c, t] for c in range(3)] + [forcing[3, t]]
                resid = residual(
                    now,
                    [lefts[s, i, c, part] for c in range(4)],
                    [rights[s, i, c, part] for c in range(4)],
                    base,
                    coef[0],
                    coef,
                )
                change = corrections(resid, lhs, mask)
                for g in range(4):
                    for c in range(4):
                        value = now[c][g] + change[g][c]
                        if s == 1:
                            smoothed[c, t, g] = value
                            continue
                        buf1[c, t + 1, g] = value
                        if g == 0:
                            outl[i, c, part] = value[0:4]
                        if g == 3:
                            outr[i, c, part] = value[4:8]
            if s == 0:
                start_chunk(1, i)

                @pl.when(jnp.logical_and(i == 0, has_after))
                def _():
                    later[1].start()

            return carry

        lax.fori_loop(0, 4, sweep, 0)

    plains = []
    for c in range(4):
        plain, ramp = time_sums(lambda t, c=c: smoothed[c, t])
        near, far = weigh(plain, ramp)
        plains.append(plain * (1.0 / 1024.0))
        for half, value in enumerate((near, far)):
            weighted[half, c] = value
            gout[0, half, c] = value[0, 0:4]
            gout[1, half, c] = value[3, 4:8]
    g_left = remote(gout.at[0], gin.at[1], gsend_sem.at[0], grecv_sem.at[1], to_left)
    g_right = remote(gout.at[1], gin.at[0], gsend_sem.at[1], grecv_sem.at[0], to_right)
    pl.when(has_left)(g_left.start)
    pl.when(has_right)(g_right.start)

    nothing = [jnp.zeros((4, 128), F32)] * 4
    for half in range(2):
        now = [weighted[half, c] for c in range(4)]
        mass = [-p for p in plains] if half == 0 else plains
        base = [weighted_f[half, c] + (mass[c] if c < 3 else 0.0) for c in range(4)]
        resid = residual(now, nothing, nothing, base, coef[7], coef)
        for c in range(4):
            row = 4 * half + c
            for g in range(4):
                parts[pl.ds(64 * g + row, 8, stride=8), :] = resid[c][g]
            edge[pl.ds(row, 4, stride=8), :] = resid[c][0, 0:4]
            edge[pl.ds(32 + row, 4, stride=8), :] = resid[c][3, 4:8]

    def tile(ref, row):
        return ref.at[pl.ds(pl.multiple_of(row * 8, 8), 8)]

    def piece(ref, row, peer):
        return remote(tile(ref, row), recv.at[tb], psend_sem, precv_sem, {"tm": peer})

    def send_inner(step, carry):
        peer = 4 + lax.rem(tb + step, 24)
        pl.when(peer != tb)(piece(parts, peer, peer).start)
        return carry

    lax.fori_loop(0, 24, send_inner, 0)

    @pl.when(jnp.logical_and(tb >= 4, tb < 28))
    def _():
        recv[tb] = tile(parts, tb)[...]

    def add_edge(side, at, coefs, g, rows, sign):
        for half in range(2):
            near = [gin[side, half, c] for c in range(4)]
            for c in range(4):
                if c < 3:
                    extra = coef[coefs, g][rows] * near[c]
                    if c == 0:
                        extra = extra - sign * 0.5 * near[3]
                else:
                    extra = STABILIZE * near[3] + sign * 0.5 * near[0]
                where = pl.ds(at + 4 * half + c, 4, stride=8)
                edge[where, :] = edge[where, :] + extra

    @pl.when(has_left)
    def _():
        g_right.wait_recv()
        add_edge(0, 0, 1, 0, slice(0, 4), -1.0)

    @pl.when(has_right)
    def _():
        g_left.wait_recv()
        add_edge(1, 32, 2, 3, slice(4, 8), 1.0)

    def send_edge(step, carry):
        place = lax.rem(tb + step, 8)
        peer = place + 24 * (place // 4)
        pl.when(peer != tb)(piece(edge, place, peer).start)
        return carry

    lax.fori_loop(0, 8, send_edge, 0)

    @pl.when(tb < 4)
    def _():
        recv[tb] = tile(edge, tb)[...]

    @pl.when(tb >= 28)
    def _():
        recv[tb] = tile(edge, tb - 24)[...]

    @pl.when(has_left)
    def _():
        remote(rights, rights, send_sem.at[0], recv_sem.at[0, 1, 0], to_left).wait_send()
        v_left.wait_send()
        g_left.wait_send()

    @pl.when(has_right)
    def _():
        remote(lefts, lefts, send_sem.at[1], recv_sem.at[0, 0, 0], to_right).wait_send()
        v_right.wait_send()
        g_right.wait_send()

    @pl.when(has_after)
    def _():
        later[0].wait_send()
        later[1].wait_send()

    pieces = remote(recv.at[0:31], recv.at[0:31], psend_sem, precv_sem, {"tm": tb})
    pieces.wait_send()
    pieces.wait_recv()
    before = jnp.zeros((4, 128), F32)
    for k in range(8):
        block = (recv[4 * k] + recv[4 * k + 1]) + (recv[4 * k + 2] + recv[4 * k + 3])
        level = block[0:4] + before
        before = block[4:8]
        for c in range(4):
            coarse[c, k : k + 1, :] = level[c : c + 1]


def per_device(initial_guess, forcing, visc_table, visc_class, inverse_bank, patch_kind):
    hbm = pl.BlockSpec(memory_space=pltpu.HBM)
    vmem = pl.BlockSpec(memory_space=pltpu.VMEM)
    dma = pltpu.SemaphoreType.DMA
    smoothed, coarse = pl.pallas_call(
        kernel,
        out_shape=(
            pltpu.VMEM((4, 8, 4, 8, 128), F32),
            pltpu.VMEM((4, 8, 128), F32),
        ),
        in_specs=[hbm] * 7,
        out_specs=(vmem, vmem),
        scratch_shapes=[
            pltpu.SMEM((8,), F32),
            pltpu.VMEM((4, 8, 128), jnp.int32),
            pltpu.VMEM((4, 32, 32), BF16),
            pltpu.VMEM((4, 2, 64), jnp.int32),
            pltpu.VMEM((4, 9, 4, 8, 128), F32),
            pltpu.VMEM((4, 9, 4, 8, 128), F32),
            pltpu.VMEM((4, 8, 4, 8, 128), F32),
            pltpu.VMEM((2, 4, 4, 2, 4, 128), F32),
            pltpu.VMEM((2, 4, 4, 2, 4, 128), F32),
            pltpu.VMEM((4, 4, 2, 4, 128), F32),
            pltpu.VMEM((4, 4, 2, 4, 128), F32),
            pltpu.VMEM((2, 4, 128), F32),
            pltpu.VMEM((2, 4, 128), F32),
            pltpu.VMEM((8, 4, 8, 128), F32),
            pltpu.VMEM((64, 256), BF16),
            pltpu.VMEM((4, 4, 16, 128), BF16),
            pltpu.VMEM((2, 4, 4, 8, 128), F32),
            pltpu.VMEM((2, 4, 4, 8, 128), F32),
            pltpu.VMEM((2, 2, 4, 4, 128), F32),
            pltpu.VMEM((2, 2, 4, 4, 128), F32),
            pltpu.VMEM((256, 128), F32),
            pltpu.VMEM((64, 128), F32),
            pltpu.VMEM((32, 8, 128), F32),
            dma((6,)),
            dma((2,)),
            dma((2, 2, 4)),
            dma((2,)),
            dma((2,)),
            dma((2,)),
            dma((2,)),
            dma((2,)),
            dma((2,)),
            dma,
            dma,
        ],
        compiler_params=pltpu.CompilerParams(
            collective_id=0, has_side_effects=True, vmem_limit_bytes=60 * 1024 * 1024
        ),
    )(
        initial_guess,
        initial_guess.reshape(4, 8, 4, 8, 128),
        forcing.reshape(4, 8, 4, 8, 128),
        visc_table,
        visc_class.reshape(4, 8, 128),
        inverse_bank,
        patch_kind,
    )
    return smoothed.reshape(4, 8, 8, 4, 128), coarse


def solution(mesh):
    return jax.shard_map(
        per_device,
        mesh=mesh,
        in_specs=(
            P(None, "tm", "space", None, None),
            P(None, "tm", "space", None, None),
            P(),
            P("space", None, None),
            P(),
            P("space", None, None),
        ),
        out_specs=(P(None, "tm", "space", None, None), P(None, None, ("space", "tm"))),
        check_vma=False,
    )
```

time: 44 us -> 32.8 us (0.75)
  Pallas kernels: 37.2 us -> 30.7 us
  local copies, waits for them, and re-layouts: 5.63 us -> 1.4 us
    pallas_call x1, Pallas kernels: 37.2 us -> 30.7 us  [per_device(): pl.pallas_call(kernel, out_shape=(pltpu.VMEM((4, 8, 4, 8, 128), F32), plt...]
    unnamed x14 -> x2, local copies, waits for them, and re-layouts: 5.63 us -> 1.4 us
where the time goes in v2:
time: 32.8 us; the launch traced here: 32.7 us
  Pallas kernels  30.7 us (94%)
  local copies, waits for them, and re-layouts  1.4 us (4%)
  between operations  0.64 us (2%)
    pallas_call x1, Pallas kernels, per_device(): pl.pallas_call(kernel, out_shape=(pltpu.VMEM((4, 8, 4, 8, 128), F32), plt...  30.7 us
    unnamed x2, local copies, waits for them, and re-layouts  1.4 us

profile of v2, /device:TPU:5, one launch (start us, length us, event | category | flops | bytes accessed | tf_op | source)
XLA Modules:
  0.0 32.7 jit_solution(16184131823923202462)
XLA Ops:
  0.6 30.7 %shard_map.77 = (f32[4,8,4,8,128]{4,3,2,1,0:T(8,128)S(1)}, f32[4,8,128]{2,1,0:T(8,128)S(1)}) custom-call(f32[4,8,8,4,128]{4,3,2,1,0:T(4,128)} %init5.1, f32[4,8,4,8,128]{4,3,2,1,0:T(8,128)} %bitcast.5, f32[4,8,4,8,128]{4,3,2,1,0:T(8,128)} %bitcast.6, f32[8]{0:T(128)} %table_in.1, s32[4,8,128]{2,1,0:T(8,128)} %bitcast.7, bf16[4,32,32]{2,1,0:T(8,128)(2,1)} %bank_in.1, ...), custom_call_target="tpu_custom_call" | custom-call | tf_op jit(solution)/shard_map/pallas_call | solution.py:456
  31.3 0.8 %copy.10 = f32[4,8,8,4,128]{4,3,2,1,0:T(4,128)} copy(f32[4,8,8,4,128]{4,3,2,1,0:T(4,128)S(1)} %bitcast.4) | data formatting | bytes 1048576
  32.1 0.6 %copy.11 = f32[4,8,128]{2,1,0:T(8,128)} copy(f32[4,8,128]{2,1,0:T(8,128)S(1)} %get-tuple-element.7) | data formatting | bytes 32768

commit v3 on v2

v3 whole, which is shorter than its diff:
```python
import functools

import jax
import jax.numpy as jnp
from jax import lax
from jax.experimental import pallas as pl
from jax.experimental.pallas import tpu as pltpu
from jax.sharding import PartitionSpec as P

MESH = pl.DeviceIdType.MESH
F32 = jnp.float32
BF16 = jnp.bfloat16
DAMPING = 0.8
STABILIZE = 0.1


def iota(shape, dim):
    return lax.broadcasted_iota(jnp.int32, shape, dim)


def cell_index(q):
    return (q // 8) * 8 + (q // 4 % 2) * 4 + (q % 2) * 2


def build_bank(bank_ref, lhs_ref):
    j = iota((32, 64), 0)
    q = iota((32, 64), 1)
    spread = (j == cell_index(q % 32) + q // 32).astype(BF16)
    p = iota((64, 32), 0)
    i = iota((64, 32), 1)
    gather = (i == cell_index(p % 32) + p // 32).astype(BF16)
    same = (iota((64, 64), 0) // 2 % 2) == (iota((64, 64), 1) // 2 % 2)
    wide = jnp.dot(bank_ref[...].reshape(128, 32), spread, preferred_element_type=F32).astype(BF16)
    parts = []
    for kind in range(4):
        part = jnp.dot(gather, wide[32 * kind : 32 * kind + 32], preferred_element_type=F32)
        parts.append(jnp.where(same, part, 0.0).astype(BF16))
    lhs_ref[...] = jnp.concatenate(parts, axis=1)


def kind_maps(kind_ref):
    upper = iota((8, 64), 0) // 2 % 2 == 0
    double = (iota((64, 128), 0) == iota((64, 128), 1) // 2).astype(BF16)
    maps = []
    for g in range(4):
        pair = kind_ref[g].astype(F32)
        rows = jnp.where(upper, pair[0:1], pair[1:2]).astype(BF16)
        maps.append(jnp.dot(rows, double, preferred_element_type=F32))
    return maps


def store_mask(kinds, mask_ref, at):
    for kind in range(4):
        mask = (kinds == float(kind)).astype(F32)
        mask_ref[at, kind] = jnp.concatenate([mask, mask], axis=0).astype(BF16)


def shift_x(values, left, right):
    first = jnp.concatenate([left, values[0, 0:4]], axis=0)
    last = jnp.concatenate([values[3, 4:8], right], axis=0)
    low = iota((3, 8, 128), 1) < 4
    inner = pltpu.roll(jnp.where(low, values[1:4], values[0:3]), 4, 1)
    return (
        jnp.concatenate([first[None], inner], axis=0),
        jnp.concatenate([inner, last[None]], axis=0),
    )


def shifts_yz(values):
    return (
        pltpu.roll(values, 1, 1),
        pltpu.roll(values, 7, 1),
        pltpu.roll(values, 1, 2),
        pltpu.roll(values, 127, 2),
    )


def edge_masks():
    y = iota((4, 8, 128), 1) % 4
    z = iota((4, 8, 128), 2)
    return y != 0, y != 3, z != 0, z != 127


def build_coefficients(viscosity, coef_ref):
    none = jnp.zeros((4, 128), F32)
    xm, xp = shift_x(viscosity, none, none)
    ym, yp, zm, zp = shifts_yz(viscosity)
    g, row = iota((4, 8, 128), 0), iota((4, 8, 128), 1)
    has_xm = jnp.logical_or(g > 0, row >= 4)
    has_xp = jnp.logical_or(g < 3, row < 4)
    total = jnp.zeros_like(viscosity)
    for n, (near, mask) in enumerate(zip((xm, xp, ym, yp, zm, zp), (has_xm, has_xp) + edge_masks())):
        near = jnp.where(mask, near, 0.0)
        kappa = 0.5 * (viscosity + near)
        inner = jnp.where(mask, kappa, 0.0)
        total = total + (inner if n < 2 else kappa)
        coef_ref[1 + n] = inner
    coef_ref[0] = total + 1.0
    coef_ref[7] = total


def residual(now, left, right, base, diagonal, coef_ref):
    mym, myp, mzm, mzp = edge_masks()
    pressure = now[3]
    pxm, pxp = shift_x(pressure, left[3], right[3])
    pym, pyp, pzm, pzp = shifts_yz(pressure)
    pym = jnp.where(mym, pym, 0.0)
    pyp = jnp.where(myp, pyp, 0.0)
    pzm = jnp.where(mzm, pzm, 0.0)
    pzp = jnp.where(mzp, pzp, 0.0)
    gradients = (pxp - pxm, pyp - pym, pzp - pzm)
    out = []
    divergence = None
    for c in range(3):
        value = now[c]
        xm, xp = shift_x(value, left[c], right[c])
        ym, yp, zm, zp = shifts_yz(value)
        flow = coef_ref[1] * xm + coef_ref[2] * xp
        flow = flow + (coef_ref[3] * ym + coef_ref[4] * yp)
        flow = flow + (coef_ref[5] * zm + coef_ref[6] * zp)
        out.append(base[c] - diagonal * value + flow - 0.5 * gradients[c])
        if c == 0:
            divergence = xp - xm
        elif c == 1:
            divergence = divergence + (jnp.where(myp, yp, 0.0) - jnp.where(mym, ym, 0.0))
        else:
            divergence = divergence + (jnp.where(mzp, zp, 0.0) - jnp.where(mzm, zm, 0.0))
    around = (pxm + pxp) + (pym + pyp) + (pzm + pzp)
    out.append(base[3] - STABILIZE * (6.0 * pressure - around) + 0.5 * divergence)
    return out


def face(near, own, kappa, sign):
    out = []
    for c in range(3):
        out.append(kappa * (near[c] if own is None else near[c] - own[c]))
    out[0] = out[0] - (0.5 * sign) * near[3]
    out.append(STABILIZE * near[3] + (0.5 * sign) * near[0])
    return out


def low(rows):
    return jnp.concatenate([rows, jnp.zeros((4, 128), F32)], axis=0)


def high(rows):
    return jnp.concatenate([jnp.zeros((4, 128), F32), rows], axis=0)


def corrections(units, at, lhs_ref, mask_ref):
    even = iota((8, 128), 1) % 2 == 0
    columns = []
    for unit, place in zip(units, at):
        evens = [jnp.where(even, v, pltpu.roll(v, 1, 1)) for v in unit]
        odds = [jnp.where(even, pltpu.roll(v, 127, 1), v) for v in unit]
        stack = jnp.concatenate(evens + odds, axis=0).astype(BF16).reshape(4, 16, 128)
        masked = [(stack * mask_ref[place, kind]).reshape(64, 128) for kind in range(4)]
        columns.append(jnp.concatenate(masked, axis=0))
    product = jnp.dot(
        lhs_ref[...], jnp.concatenate(columns, axis=1), preferred_element_type=F32
    )
    out = []
    for n in range(len(units)):
        across = slice(128 * n, 128 * n + 128)
        out.append(
            [
                DAMPING
                * jnp.where(even, product[8 * c : 8 * c + 8, across], product[32 + 8 * c : 40 + 8 * c, across])
                for c in range(4)
            ]
        )
    return out


def time_sums(load):
    plain = load(0)
    ramp = None
    for t in range(1, 8):
        value = load(t)
        plain = plain + value
        ramp = value * float(t) if ramp is None else ramp + value * float(t)
    return plain, ramp


def steps(body):
    def several(i, carry):
        for j in range(4):
            body(4 * i + j, i, j)
        return carry

    lax.fori_loop(0, 2, several, 0)


def kernel(
    init5, init, forc, table_in, vclass_in, bank_in, kind_in,
    smoothed, coarse, table, vclass, bank, kind,
    f0, f1, forcing, part, part2, e0, e1, lp, rp, lp2, rp2, lres, rres, ares, lcor, rcor, vk_out, vk_in,
    faces, coef, lhs, mask, weighted_f, parts, edges, recv, recv_e,
    load_sem, send_sem, recv_sem, psend_sem, precv_sem, esend_sem, erecv_sem,
):
    sx = lax.axis_index("space")
    tb = lax.axis_index("tm")
    has_left, has_right = sx > 0, sx < 7
    has_before, has_after = tb > 0, tb < 31
    is_edge = jnp.logical_or(jnp.logical_and(tb < 4, has_left), jnp.logical_and(tb >= 28, has_right))
    to_left, to_right, to_after = {"space": sx - 1}, {"space": sx + 1}, {"tm": tb + 1}
    left_after, right_after = {"space": sx - 1, "tm": tb + 1}, {"space": sx + 1, "tm": tb + 1}
    left_before, right_before = {"space": sx - 1, "tm": tb - 1}, {"space": sx + 1, "tm": tb - 1}
    both = jnp.logical_and

    barrier = pltpu.get_barrier_semaphore()

    def greet(condition, device):
        @pl.when(condition)
        def _():
            pl.semaphore_signal(barrier, inc=1, device_id=device, device_id_type=MESH)

    greet(has_left, to_left)
    greet(has_right, to_right)
    greet(both(has_left, has_before), left_before)
    greet(both(has_right, has_before), right_before)

    def greet_peer(step, carry):
        greet(True, {"tm": lax.rem(tb + step, 32)})
        return carry

    lax.fori_loop(1, 32, greet_peer, 0)

    def greet_edge(step, carry):
        peer = lax.rem(tb + step, 32)
        greet(both(tb < 4, has_left), {"space": sx - 1, "tm": peer})
        greet(both(tb >= 28, has_right), {"space": sx + 1, "tm": peer})
        return carry

    lax.fori_loop(0, 32, greet_edge, 0)

    loads = [
        pltpu.make_async_copy(table_in, table, load_sem.at[0]),
        pltpu.make_async_copy(vclass_in, vclass, load_sem.at[1]),
        pltpu.make_async_copy(kind_in, kind, load_sem.at[2]),
        pltpu.make_async_copy(init, f0, load_sem.at[3]),
        pltpu.make_async_copy(forc, forcing, load_sem.at[4]),
        pltpu.make_async_copy(bank_in, bank, load_sem.at[5]),
    ]
    for copy in loads:
        copy.start()

    @pl.when(sx == 0)
    def _():
        vk_in[0] = jnp.zeros((16, 128), F32)
        lp[...] = jnp.zeros_like(lp)
        lres[...] = jnp.zeros_like(lres)

    @pl.when(sx == 7)
    def _():
        vk_in[1] = jnp.zeros((16, 128), F32)
        rp[...] = jnp.zeros_like(rp)
        rres[...] = jnp.zeros_like(rres)

    @pl.when(tb == 0)
    def _():
        e0[...] = jnp.zeros_like(e0)
        ares[...] = jnp.zeros_like(ares)

    @pl.when(jnp.logical_or(tb == 0, sx == 0))
    def _():
        lcor[...] = jnp.zeros_like(lcor)

    @pl.when(jnp.logical_or(tb == 0, sx == 7))
    def _():
        rcor[...] = jnp.zeros_like(rcor)

    @pl.when(jnp.logical_not(is_edge))
    def _():
        recv_e[...] = jnp.zeros_like(recv_e)

    loads[0].wait()
    loads[1].wait()
    viscosity = jnp.zeros((4, 8, 128), F32)
    for label in range(8):
        viscosity = jnp.where(vclass[...] == label, table[label], viscosity)
    build_coefficients(viscosity, coef)
    loads[2].wait()
    maps = kind_maps(kind)
    vk_out[0, 0:4] = viscosity[0, 0:4]
    vk_out[1, 0:4] = viscosity[3, 4:8]
    vk_out[0, 4:8] = jnp.zeros((4, 128), F32)
    vk_out[1, 4:8] = jnp.zeros((4, 128), F32)
    vk_out[0, 8:16] = maps[0]
    vk_out[1, 8:16] = maps[3]
    for g in range(4):
        store_mask(maps[g], mask, g + 1)
    loads[3].wait()
    loads[4].wait()

    nothing = [jnp.zeros((4, 128), F32)] * 4

    def local(t, i, j):
        now = [f0[c, t] for c in range(4)]
        base = [forcing[c, t] for c in range(4)]
        for c in range(3):
            base[c] = base[c] + (f0[c, t - 1] if j else jnp.where(i > 0, f0[c, jnp.maximum(t - 1, 0)], 0.0))
        for c, value in enumerate(residual(now, nothing, nothing, base, coef[0], coef)):
            part[c, t] = value

    steps(local)

    one = lambda condition: condition.astype(jnp.int32)
    pl.semaphore_wait(
        barrier,
        31 + 5 * one(has_left) + 5 * one(has_right)
        + one(both(has_left, has_after)) + one(both(has_right, has_after)),
    )

    def remote(condition, awaited, source, target, n, device):
        copy = pltpu.make_async_remote_copy(
            source, target, send_sem.at[n], recv_sem.at[n], device_id=device, device_id_type=MESH
        )
        return condition, awaited, copy

    round_one = [
        remote(has_left, has_right, vk_out.at[0], vk_in.at[1], 0, to_left),
        remote(has_right, has_left, vk_out.at[1], vk_in.at[0], 1, to_right),
        remote(has_left, has_right, init5.at[:, :, 0], rp, 2, to_left),
        remote(has_right, has_left, init5.at[:, :, 7], lp, 3, to_right),
        remote(has_after, has_before, init.at[0:3, 7], e0, 4, to_after),
        remote(has_after, has_before, part.at[:, 7], ares, 5, to_after),
        remote(both(has_left, has_after), both(has_right, has_before), init.at[:, 7, 0], rcor, 6, left_after),
        remote(both(has_right, has_after), both(has_left, has_before), init.at[:, 7, 3], lcor, 7, right_after),
        remote(has_left, has_right, part.at[:, 0:4, 0], rres.at[:, 0:4], 8, to_left),
        remote(has_right, has_left, part.at[:, 0:4, 3], lres.at[:, 0:4], 9, to_right),
        remote(has_left, has_right, part.at[:, 4:8, 0], rres.at[:, 4:8], 10, to_left),
        remote(has_right, has_left, part.at[:, 4:8, 3], lres.at[:, 4:8], 11, to_right),
    ]
    for condition, _, copy in round_one:
        pl.when(condition)(copy.start)

    def arrive(first, last):
        for _, awaited, copy in round_one[first:last]:
            pl.when(awaited)(copy.wait_recv)

    loads[5].wait()
    build_bank(bank, lhs)
    first = (lax.rem(tb, 4) * 8).astype(F32) * (1.0 / 1024.0)

    def weigh(plain, ramp):
        far = first * plain + ramp * (1.0 / 1024.0)
        return plain * (1.0 / 32.0) - far, far

    for c in range(4):
        near, far = weigh(*time_sums(lambda t, c=c: forcing[c, t]))
        weighted_f[0, c] = near
        weighted_f[1, c] = far

    for pair in ((1, 2), (3, 4), (5, 6), (7,)):
        where = [(t, g) for t in pair for g in (1, 2)]
        units = [[part[c, t, g] for c in range(4)] for t, g in where]
        for (t, g), change in zip(where, corrections(units, [g + 1 for _, g in where], lhs, mask)):
            for c in range(4):
                f1[c, t, g] = f0[c, t, g] + change[c]

    arrive(0, 2)
    faces[0] = 0.5 * (viscosity[0, 0:4] + vk_in[0, 0:4])
    faces[1] = 0.5 * (viscosity[3, 4:8] + vk_in[1, 0:4])
    store_mask(vk_in[0, 8:16], mask, 0)
    store_mask(vk_in[1, 8:16], mask, 5)
    arrive(2, 5)

    units = [[part[c, 0, g] + (e0[c, g] if c < 3 else 0.0) for c in range(4)] for g in (1, 2)]
    for g, change in zip((1, 2), corrections(units, [2, 3], lhs, mask)):
        for c in range(4):
            f1[c, 0, g] = f0[c, 0, g] + change[c]

    def plane(ref, t, side):
        if side == 0:
            return [ref[c, t, 0, 0:4] for c in range(4)]
        return [ref[c, t, 3, 4:8] for c in range(4)]

    def outer(t, i, j):
        units = []
        for side, g, near, sign, place in ((0, 0, lp, -1.0, low), (1, 3, rp, 1.0, high)):
            extra = face([near[c, t] for c in range(4)], plane(f0, t, side), faces[side], sign)
            unit = [part[c, t, g] + place(extra[c]) for c in range(4)]
            if j == 0:
                unit = [unit[c] + jnp.where(i == 0, e0[c, g], 0.0) for c in range(3)] + unit[3:]
            units.append(unit)
        for g, change in zip((0, 3), corrections(units, [1, 4], lhs, mask)):
            for c in range(4):
                f1[c, t, g] = f0[c, t, g] + change[c]

    steps(outer)

    arrive(5, 8)
    units = [[ares[c, g] for c in range(4)] for g in range(4)]
    old = [e0[c, 0, 0:4] for c in range(3)]
    extra = face([lcor[c, 4:8] for c in range(4)], old, faces[0], -1.0)
    units[0] = [units[0][c] + low(extra[c]) for c in range(4)]
    old = [e0[c, 3, 4:8] for c in range(3)]
    extra = face([rcor[c, 0:4] for c in range(4)], old, faces[1], 1.0)
    units[3] = [units[3][c] + high(extra[c]) for c in range(4)]
    for g, change in enumerate(corrections(units, [1, 2, 3, 4], lhs, mask)):
        for c in range(3):
            e1[c, g] = e0[c, g] + change[c]

    def middle(t, i, j):
        now = [f1[c, t] for c in range(4)]
        base = [forcing[c, t] for c in range(4)]
        for c in range(3):
            if j:
                base[c] = base[c] + f1[c, t - 1]
            else:
                base[c] = base[c] + jnp.where(i > 0, f1[c, jnp.maximum(t - 1, 0)], e1[c])
        resid = residual(now, nothing, nothing, base, coef[0], coef)
        for c in range(4):
            part2[c, t] = resid[c]
        units = [[resid[c][g] for c in range(4)] for g in (1, 2)]
        for g, change in zip((1, 2), corrections(units, [2, 3], lhs, mask)):
            for c in range(4):
                smoothed[c, t, g] = now[c][g] + change[c]

    steps(middle)

    arrive(8, 12)
    for c in range(3):
        lres[c, 0] = lres[c, 0] + lcor[c]
        rres[c, 0] = rres[c, 0] + rcor[c]

    def beside(t, i, j):
        lold = [lp[c, t] for c in range(4)]
        rold = [rp[c, t] for c in range(4)]
        extra = face(plane(f0, t, 0), lold, faces[0], 1.0)
        lunit = [lres[c, t] + high(extra[c]) for c in range(4)]
        extra = face(plane(f0, t, 1), rold, faces[1], -1.0)
        runit = [rres[c, t] + low(extra[c]) for c in range(4)]
        lchange, rchange = corrections([lunit, runit], [0, 5], lhs, mask)
        for c in range(4):
            lp2[c, t] = jnp.where(has_left, lold[c] + lchange[c][4:8], 0.0)
            rp2[c, t] = jnp.where(has_right, rold[c] + rchange[c][0:4], 0.0)

    steps(beside)

    def ends(t, i, j):
        units = []
        for side, g, near, sign, place in ((0, 0, lp2, -1.0, low), (1, 3, rp2, 1.0, high)):
            extra = face([near[c, t] for c in range(4)], plane(f1, t, side), faces[side], sign)
            units.append([part2[c, t, g] + place(extra[c]) for c in range(4)])
        for g, change in zip((0, 3), corrections(units, [1, 4], lhs, mask)):
            for c in range(4):
                smoothed[c, t, g] = f1[c, t, g] + change[c]

    steps(ends)

    fields = ([], [])
    mass = []
    for c in range(4):
        plain, ramp = time_sums(lambda t, c=c: smoothed[c, t])
        near, far = weigh(plain, ramp)
        fields[0].append(near)
        fields[1].append(far)
        mass.append(plain * (1.0 / 1024.0))
    for half in range(2):
        now = fields[half]
        for side, g, sign in ((0, 0, 1.0), (1, 3, -1.0)):
            rows = slice(4 * side, 4 * side + 4)
            for c, value in enumerate(face([v[g, rows] for v in now], None, faces[side], sign)):
                edges[side, pl.ds(4 * half + c, 4, stride=8), :] = value
    for half in range(2):
        now = fields[half]
        base = [weighted_f[half, c] for c in range(4)]
        for c in range(3):
            base[c] = base[c] - mass[c] if half == 0 else base[c] + mass[c]
        resid = residual(now, nothing, nothing, base, coef[7], coef)
        for c in range(4):
            row = 4 * half + c
            for g in range(4):
                value = resid[c][g]
                if c < 3 and g == 0:
                    value = value - low(faces[0] * now[c][0, 0:4])
                if c < 3 and g == 3:
                    value = value - high(faces[1] * now[c][3, 4:8])
                parts[pl.ds(64 * g + row, 8, stride=8), :] = value

    def tile(ref, row):
        return ref.at[pl.ds(pl.multiple_of(row * 8, 8), 8)]

    def edge_piece(side, y, device):
        return pltpu.make_async_remote_copy(
            edges.at[side, pl.ds(8 * y, 8)], recv_e.at[tb], esend_sem.at[side], erecv_sem,
            device_id=device, device_id_type=MESH,
        )

    @pl.when(has_left)
    def _():
        for y in range(4):
            edge_piece(0, y, {"space": sx - 1, "tm": 28 + y}).start()

    @pl.when(has_right)
    def _():
        for y in range(4):
            edge_piece(1, y, {"space": sx + 1, "tm": y}).start()

    def send(step, carry):
        k = step // 4
        odd = lax.rem(k, 2)
        dz = 4 + (k // 2) * (1 - odd) - ((k + 1) // 2) * odd
        column = lax.rem(lax.rem(tb, 16) + 2 * dz, 16)
        column = column // 2 * 2 + lax.rem(tb + step, 2)
        peer = lax.rem(tb // 16 + 1 + lax.rem(step // 2, 2), 2) * 16 + column

        @pl.when(peer != tb)
        def _():
            pltpu.make_async_remote_copy(
                tile(parts, peer), recv.at[tb], psend_sem, precv_sem,
                device_id={"tm": peer}, device_id_type=MESH,
            ).start()

        return carry

    lax.fori_loop(0, 32, send, 0)
    recv[tb] = tile(parts, tb)[...]

    for condition, _, copy in round_one:
        pl.when(condition)(copy.wait_send)

    def sent_edges(side, device):
        pltpu.make_async_remote_copy(
            edges.at[side], edges.at[side], esend_sem.at[side], erecv_sem,
            device_id=device, device_id_type=MESH,
        ).wait_send()

    pl.when(has_left)(lambda: sent_edges(0, to_left))
    pl.when(has_right)(lambda: sent_edges(1, to_right))
    pieces = pltpu.make_async_remote_copy(
        recv.at[0:31], recv.at[0:31], psend_sem, precv_sem, device_id=to_after, device_id_type=MESH
    )
    pieces.wait_send()
    pieces.wait_recv()

    @pl.when(is_edge)
    def _():
        pltpu.make_async_remote_copy(
            recv_e, recv_e, psend_sem, erecv_sem, device_id=to_after, device_id_type=MESH
        ).wait_recv()

    before = jnp.zeros((4, 128), F32)
    for k in range(8):
        block = (recv[4 * k] + recv[4 * k + 1]) + (recv[4 * k + 2] + recv[4 * k + 3])
        block = block + (
            (recv_e[4 * k] + recv_e[4 * k + 1]) + (recv_e[4 * k + 2] + recv_e[4 * k + 3])
        )
        level = block[0:4] + before
        before = block[4:8]
        for c in range(4):
            coarse[c, k : k + 1, :] = level[c : c + 1]


def per_device(initial_guess, forcing, visc_table, visc_class, inverse_bank, patch_kind):
    hbm = pl.BlockSpec(memory_space=pltpu.HBM)
    vmem = pl.BlockSpec(memory_space=pltpu.VMEM)
    dma = pltpu.SemaphoreType.DMA
    smoothed, coarse = pl.pallas_call(
        kernel,
        out_shape=(
            pltpu.VMEM((4, 8, 4, 8, 128), F32),
            pltpu.VMEM((4, 8, 128), F32),
        ),
        in_specs=[hbm] * 7,
        out_specs=(vmem, vmem),
        scratch_shapes=[
            pltpu.SMEM((8,), F32),
            pltpu.VMEM((4, 8, 128), jnp.int32),
            pltpu.VMEM((4, 32, 32), BF16),
            pltpu.VMEM((4, 2, 64), jnp.int32),
            pltpu.VMEM((4, 8, 4, 8, 128), F32),
            pltpu.VMEM((4, 8, 4, 8, 128), F32),
            pltpu.VMEM((4, 8, 4, 8, 128), F32),
            pltpu.VMEM((4, 8, 4, 8, 128), F32),
            pltpu.VMEM((4, 8, 4, 8, 128), F32),
            pltpu.VMEM((3, 4, 8, 128), F32),
            pltpu.VMEM((3, 4, 8, 128), F32),
            pltpu.VMEM((4, 8, 4, 128), F32),
            pltpu.VMEM((4, 8, 4, 128), F32),
            pltpu.VMEM((4, 8, 4, 128), F32),
            pltpu.VMEM((4, 8, 4, 128), F32),
            pltpu.VMEM((4, 8, 8, 128), F32),
            pltpu.VMEM((4, 8, 8, 128), F32),
            pltpu.VMEM((4, 4, 8, 128), F32),
            pltpu.VMEM((4, 8, 128), F32),
            pltpu.VMEM((4, 8, 128), F32),
            pltpu.VMEM((2, 16, 128), F32),
            pltpu.VMEM((2, 16, 128), F32),
            pltpu.VMEM((2, 4, 128), F32),
            pltpu.VMEM((8, 4, 8, 128), F32),
            pltpu.VMEM((64, 256), BF16),
            pltpu.VMEM((6, 4, 16, 128), BF16),
            pltpu.VMEM((2, 4, 4, 8, 128), F32),
            pltpu.VMEM((256, 128), F32),
            pltpu.VMEM((2, 32, 128), F32),
            pltpu.VMEM((32, 8, 128), F32),
            pltpu.VMEM((32, 8, 128), F32),
            dma((6,)),
            dma((12,)),
            dma((12,)),
            dma,
            dma,
            dma((2,)),
            dma,
        ],
        compiler_params=pltpu.CompilerParams(
            collective_id=0, has_side_effects=True, vmem_limit_bytes=60 * 1024 * 1024
        ),
    )(
        initial_guess,
        initial_guess.reshape(4, 8, 4, 8, 128),
        forcing.reshape(4, 8, 4, 8, 128),
        visc_table,
        visc_class.reshape(4, 8, 128),
        inverse_bank,
        patch_kind,
    )
    return smoothed.reshape(4, 8, 8, 4, 128), coarse


def solution(mesh):
    return jax.shard_map(
        per_device,
        mesh=mesh,
        in_specs=(
            P(None, "tm", "space", None, None),
            P(None, "tm", "space", None, None),
            P(),
            P("space", None, None),
            P(),
            P("space", None, None),
        ),
        out_specs=(P(None, "tm", "space", None, None), P(None, None, ("space", "tm"))),
        check_vma=False,
    )
```

time: 32.8 us -> 30.4 us (0.927)
  Pallas kernels: 30.7 us -> 28.3 us
    pallas_call x1, Pallas kernels: 30.7 us -> 28.3 us  [per_device(): pl.pallas_call(kernel, out_shape=(pltpu.VMEM((4, 8, 4, 8, 128), F32), plt...]
where the time goes in v3:
time: 30.4 us; the launch traced here: 30.3 us
  Pallas kernels  28.3 us (93%)
  local copies, waits for them, and re-layouts  1.4 us (5%)
  between operations  0.64 us (2%)
    pallas_call x1, Pallas kernels, per_device(): pl.pallas_call(kernel, out_shape=(pltpu.VMEM((4, 8, 4, 8, 128), F32), plt...  28.3 us
    unnamed x2, local copies, waits for them, and re-layouts  1.4 us

profile of v3, /device:TPU:5, one launch (start us, length us, event | category | flops | bytes accessed | tf_op | source)
XLA Modules:
  0.0 30.3 jit_solution(17611175775021338507)
XLA Ops:
  0.6 28.3 %shard_map.77 = (f32[4,8,4,8,128]{4,3,2,1,0:T(8,128)S(1)}, f32[4,8,128]{2,1,0:T(8,128)S(1)}) custom-call(f32[4,8,8,4,128]{4,3,2,1,0:T(4,128)} %init5.1, f32[4,8,4,8,128]{4,3,2,1,0:T(8,128)} %bitcast.5, f32[4,8,4,8,128]{4,3,2,1,0:T(8,128)} %bitcast.6, f32[8]{0:T(128)} %table_in.1, s32[4,8,128]{2,1,0:T(8,128)} %bitcast.7, bf16[4,32,32]{2,1,0:T(8,128)(2,1)} %bank_in.1, ...), custom_call_target="tpu_custom_call" | custom-call | tf_op jit(solution)/shard_map/pallas_call | solution.py:561
  28.9 0.8 %copy.10 = f32[4,8,8,4,128]{4,3,2,1,0:T(4,128)} copy(f32[4,8,8,4,128]{4,3,2,1,0:T(4,128)S(1)} %bitcast.4) | data formatting | bytes 1048576
  29.7 0.6 %copy.11 = f32[4,8,128]{2,1,0:T(8,128)} copy(f32[4,8,128]{2,1,0:T(8,128)S(1)} %get-tuple-element.7) | data formatting | bytes 32768

commit v4 on v3

--- a/solution.py
+++ b/solution.py
@@ -196,7 +196,7 @@
     smoothed, coarse, table, vclass, bank, kind,
     f0, f1, forcing, part, part2, e0, e1, lp, rp, lp2, rp2, lres, rres, ares, lcor, rcor, vk_out, vk_in,
     faces, coef, lhs, mask, weighted_f, parts, edges, recv, recv_e,
-    load_sem, send_sem, recv_sem, psend_sem, precv_sem, esend_sem, erecv_sem,
+    load_sem, send_sem, recv_sem, psend_sem, precv_sem, esend_sem, erecv_sem, token_sem,
 ):
     sx = lax.axis_index("space")
     tb = lax.axis_index("tm")
@@ -215,24 +215,35 @@
         def _():
             pl.semaphore_signal(barrier, inc=1, device_id=device, device_id_type=MESH)
 
+    column, row = lax.rem(tb, 16), tb // 16
+    ring = [{"tm": row * 16 + lax.rem(column + step, 16)} for step in (2, 14)]
+    across = {"tm": lax.rem(tb + 16, 32)}
+    partner = {"tm": tb + 1 - 2 * lax.rem(tb, 2)}
     greet(has_left, to_left)
     greet(has_right, to_right)
+    greet(has_before, {"tm": tb - 1})
+    greet(has_after, to_after)
     greet(both(has_left, has_before), left_before)
     greet(both(has_right, has_before), right_before)
-
-    def greet_peer(step, carry):
-        greet(True, {"tm": lax.rem(tb + step, 32)})
-        return carry
-
-    lax.fori_loop(1, 32, greet_peer, 0)
-
-    def greet_edge(step, carry):
-        peer = lax.rem(tb + step, 32)
-        greet(both(tb < 4, has_left), {"space": sx - 1, "tm": peer})
-        greet(both(tb >= 28, has_right), {"space": sx + 1, "tm": peer})
-        return carry
-
-    lax.fori_loop(0, 32, greet_edge, 0)
+    for device in ring + [across]:
+        greet(True, device)
+
+    def tell(n, devices):
+        for condition, device in devices:
+
+            @pl.when(condition)
+            def _(device=device):
+                pl.semaphore_signal(token_sem.at[n], inc=1, device_id=device, device_id_type=MESH)
+
+    circles = [[(True, device) for device in ring]] * 3
+    circles += [[(True, across)], [(True, partner)], [(has_left, to_left), (has_right, to_right)]]
+    counts = [2, 2, 2, 1, 1, has_left.astype(jnp.int32) + has_right.astype(jnp.int32)]
+
+    def pass_on(n):
+        if n > 0:
+            pl.semaphore_wait(token_sem.at[n - 1], counts[n - 1])
+        if n < 6:
+            tell(n, circles[n])
 
     loads = [
         pltpu.make_async_copy(table_in, table, load_sem.at[0]),
@@ -308,7 +319,7 @@
     one = lambda condition: condition.astype(jnp.int32)
     pl.semaphore_wait(
         barrier,
-        31 + 5 * one(has_left) + 5 * one(has_right)
+        3 + one(has_left) + one(has_right) + one(has_before) + one(has_after)
         + one(both(has_left, has_after)) + one(both(has_right, has_after)),
     )
 
@@ -334,6 +345,7 @@
     ]
     for condition, _, copy in round_one:
         pl.when(condition)(copy.start)
+    pass_on(0)
 
     def arrive(first, last):
         for _, awaited, copy in round_one[first:last]:
@@ -351,6 +363,8 @@
         near, far = weigh(*time_sums(lambda t, c=c: forcing[c, t]))
         weighted_f[0, c] = near
         weighted_f[1, c] = far
+
+    pass_on(1)
 
     for pair in ((1, 2), (3, 4), (5, 6), (7,)):
         where = [(t, g) for t in pair for g in (1, 2)]
@@ -359,12 +373,14 @@
             for c in range(4):
                 f1[c, t, g] = f0[c, t, g] + change[c]
 
+    pass_on(2)
     arrive(0, 2)
     faces[0] = 0.5 * (viscosity[0, 0:4] + vk_in[0, 0:4])
     faces[1] = 0.5 * (viscosity[3, 4:8] + vk_in[1, 0:4])
     store_mask(vk_in[0, 8:16], mask, 0)
     store_mask(vk_in[1, 8:16], mask, 5)
     arrive(2, 5)
+    pass_on(3)
 
     units = [[part[c, 0, g] + (e0[c, g] if c < 3 else 0.0) for c in range(4)] for g in (1, 2)]
     for g, change in zip((1, 2), corrections(units, [2, 3], lhs, mask)):
@@ -389,6 +405,8 @@
                 f1[c, t, g] = f0[c, t, g] + change[c]
 
     steps(outer)
+
+    pass_on(4)
 
     arrive(5, 8)
     units = [[ares[c, g] for c in range(4)] for g in range(4)]
@@ -419,6 +437,8 @@
                 smoothed[c, t, g] = now[c][g] + change[c]
 
     steps(middle)
+
+    pass_on(5)
 
     arrive(8, 12)
     for c in range(3):
@@ -488,6 +508,8 @@
             edges.at[side, pl.ds(8 * y, 8)], recv_e.at[tb], esend_sem.at[side], erecv_sem,
             device_id=device, device_id_type=MESH,
         )
+
+    pass_on(6)
 
     @pl.when(has_left)
     def _():
@@ -605,6 +627,7 @@
             dma,
             dma((2,)),
             dma,
+            pltpu.SemaphoreType.REGULAR((6,)),
         ],
         compiler_params=pltpu.CompilerParams(
             collective_id=0, has_side_effects=True, vmem_limit_bytes=60 * 1024 * 1024

time: 30.4 us -> 29.4 us (0.967)
  Pallas kernels: 28.3 us -> 27.3 us
    pallas_call x1, Pallas kernels: 28.3 us -> 27.3 us  [per_device(): pl.pallas_call(kernel, out_shape=(pltpu.VMEM((4, 8, 4, 8, 128), F32), plt...]
where the time goes in v4:
time: 29.4 us; the launch traced here: 29.3 us
  Pallas kernels  27.3 us (93%)
  local copies, waits for them, and re-layouts  1.4 us (5%)
  between operations  0.64 us (2%)
    pallas_call x1, Pallas kernels, per_device(): pl.pallas_call(kernel, out_shape=(pltpu.VMEM((4, 8, 4, 8, 128), F32), plt...  27.3 us
    unnamed x2, local copies, waits for them, and re-layouts  1.4 us

profile of v4, /device:TPU:5, one launch (start us, length us, event | category | flops | bytes accessed | tf_op | source)
XLA Modules:
  0.0 29.3 jit_solution(14469386732365539656)
XLA Ops:
  0.6 27.3 %shard_map.77 = (f32[4,8,4,8,128]{4,3,2,1,0:T(8,128)S(1)}, f32[4,8,128]{2,1,0:T(8,128)S(1)}) custom-call(f32[4,8,8,4,128]{4,3,2,1,0:T(4,128)} %init5.1, f32[4,8,4,8,128]{4,3,2,1,0:T(8,128)} %bitcast.5, f32[4,8,4,8,128]{4,3,2,1,0:T(8,128)} %bitcast.6, f32[8]{0:T(128)} %table_in.1, s32[4,8,128]{2,1,0:T(8,128)} %bitcast.7, bf16[4,32,32]{2,1,0:T(8,128)(2,1)} %bank_in.1, ...), custom_call_target="tpu_custom_call" | custom-call | tf_op jit(solution)/shard_map/pallas_call | solution.py:583
  27.9 0.8 %copy.10 = f32[4,8,8,4,128]{4,3,2,1,0:T(4,128)} copy(f32[4,8,8,4,128]{4,3,2,1,0:T(4,128)S(1)} %bitcast.4) | data formatting | bytes 1048576
  28.7 0.6 %copy.11 = f32[4,8,128]{2,1,0:T(8,128)} copy(f32[4,8,128]{2,1,0:T(8,128)S(1)} %get-tuple-element.7) | data formatting | bytes 32768

commit v5 on v4

--- a/solution.py
+++ b/solution.py
@@ -195,7 +195,7 @@
     init5, init, forc, table_in, vclass_in, bank_in, kind_in,
     smoothed, coarse, table, vclass, bank, kind,
     f0, f1, forcing, part, part2, e0, e1, lp, rp, lp2, rp2, lres, rres, ares, lcor, rcor, vk_out, vk_in,
-    faces, coef, lhs, mask, weighted_f, parts, edges, recv, recv_e,
+    faces, fields, mass, coef, lhs, mask, weighted_f, parts, edges, recv, recv_e,
     load_sem, send_sem, recv_sem, psend_sem, precv_sem, esend_sem, erecv_sem, token_sem,
 ):
     sx = lax.axis_index("space")
@@ -217,6 +217,7 @@
 
     column, row = lax.rem(tb, 16), tb // 16
     ring = [{"tm": row * 16 + lax.rem(column + step, 16)} for step in (2, 14)]
+    far_ring = [{"tm": row * 16 + lax.rem(column + step, 16)} for step in (4, 12)]
     across = {"tm": lax.rem(tb + 16, 32)}
     partner = {"tm": tb + 1 - 2 * lax.rem(tb, 2)}
     greet(has_left, to_left)
@@ -235,14 +236,19 @@
             def _(device=device):
                 pl.semaphore_signal(token_sem.at[n], inc=1, device_id=device, device_id_type=MESH)
 
-    circles = [[(True, device) for device in ring]] * 3
-    circles += [[(True, across)], [(True, partner)], [(has_left, to_left), (has_right, to_right)]]
-    counts = [2, 2, 2, 1, 1, has_left.astype(jnp.int32) + has_right.astype(jnp.int32)]
+    circles = [
+        [(True, partner)],
+        [(True, device) for device in ring],
+        [(True, device) for device in far_ring],
+        [(True, across)],
+        [(has_left, to_left), (has_right, to_right)],
+    ]
+    counts = [1, 2, 2, 1, has_left.astype(jnp.int32) + has_right.astype(jnp.int32)]
 
     def pass_on(n):
         if n > 0:
             pl.semaphore_wait(token_sem.at[n - 1], counts[n - 1])
-        if n < 6:
+        if n < 5:
             tell(n, circles[n])
 
     loads = [
@@ -338,11 +344,13 @@
         remote(has_after, has_before, part.at[:, 7], ares, 5, to_after),
         remote(both(has_left, has_after), both(has_right, has_before), init.at[:, 7, 0], rcor, 6, left_after),
         remote(both(has_right, has_after), both(has_left, has_before), init.at[:, 7, 3], lcor, 7, right_after),
-        remote(has_left, has_right, part.at[:, 0:4, 0], rres.at[:, 0:4], 8, to_left),
-        remote(has_right, has_left, part.at[:, 0:4, 3], lres.at[:, 0:4], 9, to_right),
-        remote(has_left, has_right, part.at[:, 4:8, 0], rres.at[:, 4:8], 10, to_left),
-        remote(has_right, has_left, part.at[:, 4:8, 3], lres.at[:, 4:8], 11, to_right),
     ]
+    for i in range(2):
+        pair = slice(4 * i, 4 * i + 4)
+        round_one += [
+            remote(has_left, has_right, part.at[:, pair, 0], rres.at[:, pair], 8 + 2 * i, to_left),
+            remote(has_right, has_left, part.at[:, pair, 3], lres.at[:, pair], 9 + 2 * i, to_right),
+        ]
     for condition, _, copy in round_one:
         pl.when(condition)(copy.start)
     pass_on(0)
@@ -353,6 +361,7 @@
 
     loads[5].wait()
     build_bank(bank, lhs)
+    pass_on(1)
     first = (lax.rem(tb, 4) * 8).astype(F32) * (1.0 / 1024.0)
 
     def weigh(plain, ramp):
@@ -364,7 +373,6 @@
         weighted_f[0, c] = near
         weighted_f[1, c] = far
 
-    pass_on(1)
 
     for pair in ((1, 2), (3, 4), (5, 6), (7,)):
         where = [(t, g) for t in pair for g in (1, 2)]
@@ -405,6 +413,7 @@
                 f1[c, t, g] = f0[c, t, g] + change[c]
 
     steps(outer)
+
 
     pass_on(4)
 
@@ -438,54 +447,80 @@
 
     steps(middle)
 
+
+    def sum_up(rows):
+        for c in range(4):
+            plain, ramp = time_sums(lambda t: smoothed[c, t, rows])
+            near, far = weigh(plain, ramp)
+            fields[0, c, rows] = near
+            fields[1, c, rows] = far
+            mass[c, rows] = plain * (1.0 / 1024.0)
+
+    sum_up(slice(1, 3))
+
+    def beside(pair):
+        units = []
+        for t in pair:
+            extra = face(plane(f0, t, 0), [lp[c, t] for c in range(4)], faces[0], 1.0)
+            unit = [lres[c, t] + high(extra[c]) for c in range(4)]
+            if t == 0:
+                unit = [unit[c] + lcor[c] for c in range(3)] + unit[3:]
+            units.append(unit)
+            extra = face(plane(f0, t, 1), [rp[c, t] for c in range(4)], faces[1], -1.0)
+            unit = [rres[c, t] + low(extra[c]) for c in range(4)]
+            if t == 0:
+                unit = [unit[c] + rcor[c] for c in range(3)] + unit[3:]
+            units.append(unit)
+        changes = corrections(units, [0, 5] * 8, lhs, mask)
+        for n, t in enumerate(pair):
+            for c in range(4):
+                lp2[c, t] = jnp.where(has_left, lp[c, t] + changes[2 * n][c][4:8], 0.0)
+                rp2[c, t] = jnp.where(has_right, rp[c, t] + changes[2 * n + 1][c][0:4], 0.0)
+
+    def ends(pair):
+        units = []
+        for t in pair:
+            for side, g, near, sign, place in ((0, 0, lp2, -1.0, low), (1, 3, rp2, 1.0, high)):
+                extra = face([near[c, t] for c in range(4)], plane(f1, t, side), faces[side], sign)
+                units.append([part2[c, t, g] + place(extra[c]) for c in range(4)])
+        changes = corrections(units, [1, 4] * 8, lhs, mask)
+        for n, t in enumerate(pair):
+            for side, g in ((0, 0), (1, 3)):
+                for c in range(4):
+                    smoothed[c, t, g] = f1[c, t, g] + changes[2 * n + side][c]
+
+    arrive(8, 12)
+    beside(range(8))
+    ends(range(8))
+
+    for g in (0, 3):
+        sum_up(slice(g, g + 1))
+    for half in range(2):
+        for side, rows, sign in ((0, slice(0, 4), 1.0), (1, slice(4, 8), -1.0)):
+            near = [fields[half, c, 3 * side, rows] for c in range(4)]
+            for c, value in enumerate(face(near, None, faces[side], sign)):
+                edges[side, pl.ds(4 * half + c, 4, stride=8), :] = value
+
+    def edge_piece(side, y, device):
+        return pltpu.make_async_remote_copy(
+            edges.at[side, pl.ds(8 * y, 8)], recv_e.at[tb], esend_sem.at[side], erecv_sem,
+            device_id=device, device_id_type=MESH,
+        )
+
     pass_on(5)
 
-    arrive(8, 12)
-    for c in range(3):
-        lres[c, 0] = lres[c, 0] + lcor[c]
-        rres[c, 0] = rres[c, 0] + rcor[c]
-
-    def beside(t, i, j):
-        lold = [lp[c, t] for c in range(4)]
-        rold = [rp[c, t] for c in range(4)]
-        extra = face(plane(f0, t, 0), lold, faces[0], 1.0)
-        lunit = [lres[c, t] + high(extra[c]) for c in range(4)]
-        extra = face(plane(f0, t, 1), rold, faces[1], -1.0)
-        runit = [rres[c, t] + low(extra[c]) for c in range(4)]
-        lchange, rchange = corrections([lunit, runit], [0, 5], lhs, mask)
-        for c in range(4):
-            lp2[c, t] = jnp.where(has_left, lold[c] + lchange[c][4:8], 0.0)
-            rp2[c, t] = jnp.where(has_right, rold[c] + rchange[c][0:4], 0.0)
-
-    steps(beside)
-
-    def ends(t, i, j):
-        units = []
-        for side, g, near, sign, place in ((0, 0, lp2, -1.0, low), (1, 3, rp2, 1.0, high)):
-            extra = face([near[c, t] for c in range(4)], plane(f1, t, side), faces[side], sign)
-            units.append([part2[c, t, g] + place(extra[c]) for c in range(4)])
-        for g, change in zip((0, 3), corrections(units, [1, 4], lhs, mask)):
-            for c in range(4):
-                smoothed[c, t, g] = f1[c, t, g] + change[c]
-
-    steps(ends)
-
-    fields = ([], [])
-    mass = []
-    for c in range(4):
-        plain, ramp = time_sums(lambda t, c=c: smoothed[c, t])
-        near, far = weigh(plain, ramp)
-        fields[0].append(near)
-        fields[1].append(far)
-        mass.append(plain * (1.0 / 1024.0))
+    @pl.when(has_left)
+    def _():
+        for y in range(4):
+            edge_piece(0, y, {"space": sx - 1, "tm": 28 + y}).start()
+
+    @pl.when(has_right)
+    def _():
+        for y in range(4):
+            edge_piece(1, y, {"space": sx + 1, "tm": y}).start()
+
     for half in range(2):
-        now = fields[half]
-        for side, g, sign in ((0, 0, 1.0), (1, 3, -1.0)):
-            rows = slice(4 * side, 4 * side + 4)
-            for c, value in enumerate(face([v[g, rows] for v in now], None, faces[side], sign)):
-                edges[side, pl.ds(4 * half + c, 4, stride=8), :] = value
-    for half in range(2):
-        now = fields[half]
+        now = [fields[half, c] for c in range(4)]
         base = [weighted_f[half, c] for c in range(4)]
         for c in range(3):
             base[c] = base[c] - mass[c] if half == 0 else base[c] + mass[c]
@@ -503,24 +538,6 @@
     def tile(ref, row):
         return ref.at[pl.ds(pl.multiple_of(row * 8, 8), 8)]
 
-    def edge_piece(side, y, device):
-        return pltpu.make_async_remote_copy(
-            edges.at[side, pl.ds(8 * y, 8)], recv_e.at[tb], esend_sem.at[side], erecv_sem,
-            device_id=device, device_id_type=MESH,
-        )
-
-    pass_on(6)
-
-    @pl.when(has_left)
-    def _():
-        for y in range(4):
-            edge_piece(0, y, {"space": sx - 1, "tm": 28 + y}).start()
-
-    @pl.when(has_right)
-    def _():
-        for y in range(4):
-            edge_piece(1, y, {"space": sx + 1, "tm": y}).start()
-
     def send(step, carry):
         k = step // 4
         odd = lax.rem(k, 2)
@@ -574,6 +591,17 @@
         before = block[4:8]
         for c in range(4):
             coarse[c, k : k + 1, :] = level[c : c + 1]
+
+
+def store(smoothed_in, coarse_in, smoothed, coarse, sems):
+    copies = [
+        pltpu.make_async_copy(smoothed_in, smoothed, sems.at[0]),
+        pltpu.make_async_copy(coarse_in, coarse, sems.at[1]),
+    ]
+    for copy in copies:
+        copy.start()
+    for copy in copies:
+        copy.wait()
 
 
 def per_device(initial_guess, forcing, visc_table, visc_class, inverse_bank, patch_kind):
@@ -612,6 +640,8 @@
             pltpu.VMEM((2, 16, 128), F32),
             pltpu.VMEM((2, 16, 128), F32),
             pltpu.VMEM((2, 4, 128), F32),
+            pltpu.VMEM((2, 4, 4, 8, 128), F32),
+            pltpu.VMEM((4, 4, 8, 128), F32),
             pltpu.VMEM((8, 4, 8, 128), F32),
             pltpu.VMEM((64, 256), BF16),
             pltpu.VMEM((6, 4, 16, 128), BF16),
@@ -627,7 +657,7 @@
             dma,
             dma((2,)),
             dma,
-            pltpu.SemaphoreType.REGULAR((6,)),
+            pltpu.SemaphoreType.REGULAR((5,)),
         ],
         compiler_params=pltpu.CompilerParams(
             collective_id=0, has_side_effects=True, vmem_limit_bytes=60 * 1024 * 1024
@@ -641,6 +671,17 @@
         inverse_bank,
         patch_kind,
     )
+    smoothed, coarse = pl.pallas_call(
+        store,
+        out_shape=(
+            jax.ShapeDtypeStruct((4, 8, 4, 8, 128), F32),
+            jax.ShapeDtypeStruct((4, 8, 128), F32),
+        ),
+        in_specs=[pl.BlockSpec(memory_space=pl.ANY)] * 2,
+        out_specs=(pl.BlockSpec(memory_space=pl.ANY),) * 2,
+        scratch_shapes=[dma((2,))],
+        compiler_params=pltpu.CompilerParams(vmem_limit_bytes=4 * 1024 * 1024),
+    )(smoothed, coarse)
     return smoothed.reshape(4, 8, 8, 4, 128), coarse
 
 

time: 29.4 us -> 28.1 us (0.956)
  local copies, waits for them, and re-layouts: 1.4 us -> 0 us
    unnamed x2 -> x0, local copies, waits for them, and re-layouts: 1.4 us -> none
    pallas_call x0 -> x1, Pallas kernels: none -> 0.81 us  [per_device(): pl.pallas_call(store, out_shape=(jax.ShapeDtypeStruct((4, 8, 4, 8, 128),...]
    pallas_call x1, Pallas kernels: 27.3 us -> 26.6 us  [per_device(): pl.pallas_call(kernel, out_shape=(pltpu.VMEM((4, 8, 4, 8, 128), F32), plt...]
where the time goes in v5:
time: 28.1 us; the launch traced here: 28 us
  Pallas kernels  27.4 us (98%)
  between operations  0.64 us (2%)
    pallas_call x1, Pallas kernels, per_device(): pl.pallas_call(kernel, out_shape=(pltpu.VMEM((4, 8, 4, 8, 128), F32), plt...  26.6 us
    pallas_call x1, Pallas kernels, per_device(): pl.pallas_call(store, out_shape=(jax.ShapeDtypeStruct((4, 8, 4, 8, 128),...  0.81 us

profile of v5, /device:TPU:5, one launch (start us, length us, event | category | flops | bytes accessed | tf_op | source)
XLA Modules:
  0.0 28.0 jit_solution(2204873948303890242)
XLA Ops:
  0.6 26.6 %shard_map.77 = (f32[4,8,4,8,128]{4,3,2,1,0:T(8,128)S(1)}, f32[4,8,128]{2,1,0:T(8,128)S(1)}) custom-call(f32[4,8,8,4,128]{4,3,2,1,0:T(4,128)} %init5.1, f32[4,8,4,8,128]{4,3,2,1,0:T(8,128)} %bitcast.4, f32[4,8,4,8,128]{4,3,2,1,0:T(8,128)} %bitcast.5, f32[8]{0:T(128)} %table_in.1, s32[4,8,128]{2,1,0:T(8,128)} %bitcast.6, bf16[4,32,32]{2,1,0:T(8,128)(2,1)} %bank_in.1, ...), custom_call_target="tpu_custom_call" | custom-call | tf_op jit(solution)/shard_map/pallas_call | solution.py:611
  27.2 0.8 %shard_map.78 = (f32[4,8,4,8,128]{4,3,2,1,0:T(8,128)}, f32[4,8,128]{2,1,0:T(8,128)}) custom-call(f32[4,8,4,8,128]{4,3,2,1,0:T(8,128)S(1)} %get-tuple-element.6.smoothed_in, f32[4,8,128]{2,1,0:T(8,128)S(1)} %get-tuple-element.7.coarse_in), custom_call_target="tpu_custom_call" | custom-call | tf_op jit(solution)/shard_map/pallas_call | solution.py:674

commit v6 on v5

--- a/solution.py
+++ b/solution.py
@@ -205,7 +205,6 @@
     is_edge = jnp.logical_or(jnp.logical_and(tb < 4, has_left), jnp.logical_and(tb >= 28, has_right))
     to_left, to_right, to_after = {"space": sx - 1}, {"space": sx + 1}, {"tm": tb + 1}
     left_after, right_after = {"space": sx - 1, "tm": tb + 1}, {"space": sx + 1, "tm": tb + 1}
-    left_before, right_before = {"space": sx - 1, "tm": tb - 1}, {"space": sx + 1, "tm": tb - 1}
     both = jnp.logical_and
 
     barrier = pltpu.get_barrier_semaphore()
@@ -216,16 +215,14 @@
             pl.semaphore_signal(barrier, inc=1, device_id=device, device_id_type=MESH)
 
     column, row = lax.rem(tb, 16), tb // 16
-    ring = [{"tm": row * 16 + lax.rem(column + step, 16)} for step in (2, 14)]
-    far_ring = [{"tm": row * 16 + lax.rem(column + step, 16)} for step in (4, 12)]
+    ring = [{"tm": row * 16 + lax.rem(column + step, 16)} for step in (2, 14, 4, 12)]
+    far_ring = ring[2:]
     across = {"tm": lax.rem(tb + 16, 32)}
     partner = {"tm": tb + 1 - 2 * lax.rem(tb, 2)}
     greet(has_left, to_left)
     greet(has_right, to_right)
     greet(has_before, {"tm": tb - 1})
     greet(has_after, to_after)
-    greet(both(has_left, has_before), left_before)
-    greet(both(has_right, has_before), right_before)
     for device in ring + [across]:
         greet(True, device)
 
@@ -241,14 +238,13 @@
         [(True, device) for device in ring],
         [(True, device) for device in far_ring],
         [(True, across)],
-        [(has_left, to_left), (has_right, to_right)],
     ]
-    counts = [1, 2, 2, 1, has_left.astype(jnp.int32) + has_right.astype(jnp.int32)]
+    counts = [1, 4, 2, 1]
 
     def pass_on(n):
         if n > 0:
             pl.semaphore_wait(token_sem.at[n - 1], counts[n - 1])
-        if n < 5:
+        if n < 4:
             tell(n, circles[n])
 
     loads = [
@@ -325,8 +321,7 @@
     one = lambda condition: condition.astype(jnp.int32)
     pl.semaphore_wait(
         barrier,
-        3 + one(has_left) + one(has_right) + one(has_before) + one(has_after)
-        + one(both(has_left, has_after)) + one(both(has_right, has_after)),
+        5 + one(has_left) + one(has_right) + one(has_before) + one(has_after),
     )
 
     def remote(condition, awaited, source, target, n, device):
@@ -351,8 +346,9 @@
             remote(has_left, has_right, part.at[:, pair, 0], rres.at[:, pair], 8 + 2 * i, to_left),
             remote(has_right, has_left, part.at[:, pair, 3], lres.at[:, pair], 9 + 2 * i, to_right),
         ]
-    for condition, _, copy in round_one:
+    for condition, _, copy in round_one[:6] + round_one[8:]:
         pl.when(condition)(copy.start)
+    tell(4, [(has_before, {"tm": tb - 1})])
     pass_on(0)
 
     def arrive(first, last):
@@ -362,6 +358,13 @@
     loads[5].wait()
     build_bank(bank, lhs)
     pass_on(1)
+
+    @pl.when(has_after)
+    def _():
+        pl.semaphore_wait(token_sem.at[4], 1)
+        for condition, _, copy in round_one[6:8]:
+            pl.when(condition)(copy.start)
+
     first = (lax.rem(tb, 4) * 8).astype(F32) * (1.0 / 1024.0)
 
     def weigh(plain, ramp):
@@ -415,7 +418,25 @@
     steps(outer)
 
 
-    pass_on(4)
+    def middle(pair):
+        units = []
+        for t in pair:
+            now = [f1[c, t] for c in range(4)]
+            base = [forcing[c, t] for c in range(4)]
+            for c in range(3):
+                base[c] = base[c] + (f1[c, t - 1] if t > 0 else e1[c])
+            resid = residual(now, nothing, nothing, base, coef[0], coef)
+            for c in range(4):
+                part2[c, t] = resid[c]
+            units += [[resid[c][g] for c in range(4)] for g in (1, 2)]
+        changes = corrections(units, [2, 3] * len(pair), lhs, mask)
+        for n, t in enumerate(pair):
+            for g in (1, 2):
+                for c in range(4):
+                    smoothed[c, t, g] = f1[c, t, g] + changes[2 * n + g - 1][c]
+
+    middle((1, 2, 3))
+    middle((4, 5, 6, 7))
 
     arrive(5, 8)
     units = [[ares[c, g] for c in range(4)] for g in range(4)]
@@ -429,23 +450,7 @@
         for c in range(3):
             e1[c, g] = e0[c, g] + change[c]
 
-    def middle(t, i, j):
-        now = [f1[c, t] for c in range(4)]
-        base = [forcing[c, t] for c in range(4)]
-        for c in range(3):
-            if j:
-                base[c] = base[c] + f1[c, t - 1]
-            else:
-                base[c] = base[c] + jnp.where(i > 0, f1[c, jnp.maximum(t - 1, 0)], e1[c])
-        resid = residual(now, nothing, nothing, base, coef[0], coef)
-        for c in range(4):
-            part2[c, t] = resid[c]
-        units = [[resid[c][g] for c in range(4)] for g in (1, 2)]
-        for g, change in zip((1, 2), corrections(units, [2, 3], lhs, mask)):
-            for c in range(4):
-                smoothed[c, t, g] = now[c][g] + change[c]
-
-    steps(middle)
+    middle((0,))
 
 
     def sum_up(rows):
@@ -507,7 +512,8 @@
             device_id=device, device_id_type=MESH,
         )
 
-    pass_on(5)
+
+    pass_on(4)
 
     @pl.when(has_left)
     def _():

time: 28.1 us -> 26.9 us (0.957)
  Pallas kernels: 27.4 us -> 26.2 us
    pallas_call x1, Pallas kernels: 26.6 us -> 25.4 us  [per_device(): pl.pallas_call(kernel, out_shape=(pltpu.VMEM((4, 8, 4, 8, 128), F32), plt...]
where the time goes in v6:
time: 26.9 us; the launch traced here: 26.8 us
  Pallas kernels  26.2 us (97%)
  between operations  0.64 us (2%)
    pallas_call x1, Pallas kernels, per_device(): pl.pallas_call(kernel, out_shape=(pltpu.VMEM((4, 8, 4, 8, 128), F32), plt...  25.4 us
    pallas_call x1, Pallas kernels, per_device(): pl.pallas_call(store, out_shape=(jax.ShapeDtypeStruct((4, 8, 4, 8, 128),...  0.81 us

profile of v6, /device:TPU:5, one launch (start us, length us, event | category | flops | bytes accessed | tf_op | source)
XLA Modules:
  0.0 26.8 jit_solution(6889828091031613231)
XLA Ops:
  0.6 25.4 %shard_map.77 = (f32[4,8,4,8,128]{4,3,2,1,0:T(8,128)S(1)}, f32[4,8,128]{2,1,0:T(8,128)S(1)}) custom-call(f32[4,8,8,4,128]{4,3,2,1,0:T(4,128)} %init5.1, f32[4,8,4,8,128]{4,3,2,1,0:T(8,128)} %bitcast.4, f32[4,8,4,8,128]{4,3,2,1,0:T(8,128)} %bitcast.5, f32[8]{0:T(128)} %table_in.1, s32[4,8,128]{2,1,0:T(8,128)} %bitcast.6, bf16[4,32,32]{2,1,0:T(8,128)(2,1)} %bank_in.1, ...), custom_call_target="tpu_custom_call" | custom-call | tf_op jit(solution)/shard_map/pallas_call | solution.py:617
  26.0 0.8 %shard_map.78 = (f32[4,8,4,8,128]{4,3,2,1,0:T(8,128)}, f32[4,8,128]{2,1,0:T(8,128)}) custom-call(f32[4,8,4,8,128]{4,3,2,1,0:T(8,128)S(1)} %get-tuple-element.6.smoothed_in, f32[4,8,128]{2,1,0:T(8,128)S(1)} %get-tuple-element.7.coarse_in), custom_call_target="tpu_custom_call" | custom-call | tf_op jit(solution)/shard_map/pallas_call | solution.py:680

commit v7 on v6

--- a/solution.py
+++ b/solution.py
@@ -195,8 +195,8 @@
     init5, init, forc, table_in, vclass_in, bank_in, kind_in,
     smoothed, coarse, table, vclass, bank, kind,
     f0, f1, forcing, part, part2, e0, e1, lp, rp, lp2, rp2, lres, rres, ares, lcor, rcor, vk_out, vk_in,
-    faces, fields, mass, coef, lhs, mask, weighted_f, parts, edges, recv, recv_e,
-    load_sem, send_sem, recv_sem, psend_sem, precv_sem, esend_sem, erecv_sem, token_sem,
+    faces, fields, mass, coef, lhs, mask, weighted_f, parts, edges, parts_in, edges_in, sums, edge_sums, recv, recv_e,
+    load_sem, send_sem, recv_sem, psend_sem, precv_sem, esend_sem, erecv_sem, token_sem, pair_send, pair_recv,
 ):
     sx = lax.axis_index("space")
     tb = lax.axis_index("tm")
@@ -286,37 +286,6 @@
     @pl.when(jnp.logical_not(is_edge))
     def _():
         recv_e[...] = jnp.zeros_like(recv_e)
-
-    loads[0].wait()
-    loads[1].wait()
-    viscosity = jnp.zeros((4, 8, 128), F32)
-    for label in range(8):
-        viscosity = jnp.where(vclass[...] == label, table[label], viscosity)
-    build_coefficients(viscosity, coef)
-    loads[2].wait()
-    maps = kind_maps(kind)
-    vk_out[0, 0:4] = viscosity[0, 0:4]
-    vk_out[1, 0:4] = viscosity[3, 4:8]
-    vk_out[0, 4:8] = jnp.zeros((4, 128), F32)
-    vk_out[1, 4:8] = jnp.zeros((4, 128), F32)
-    vk_out[0, 8:16] = maps[0]
-    vk_out[1, 8:16] = maps[3]
-    for g in range(4):
-        store_mask(maps[g], mask, g + 1)
-    loads[3].wait()
-    loads[4].wait()
-
-    nothing = [jnp.zeros((4, 128), F32)] * 4
-
-    def local(t, i, j):
-        now = [f0[c, t] for c in range(4)]
-        base = [forcing[c, t] for c in range(4)]
-        for c in range(3):
-            base[c] = base[c] + (f0[c, t - 1] if j else jnp.where(i > 0, f0[c, jnp.maximum(t - 1, 0)], 0.0))
-        for c, value in enumerate(residual(now, nothing, nothing, base, coef[0], coef)):
-            part[c, t] = value
-
-    steps(local)
 
     one = lambda condition: condition.astype(jnp.int32)
     pl.semaphore_wait(
@@ -346,10 +315,56 @@
             remote(has_left, has_right, part.at[:, pair, 0], rres.at[:, pair], 8 + 2 * i, to_left),
             remote(has_right, has_left, part.at[:, pair, 3], lres.at[:, pair], 9 + 2 * i, to_right),
         ]
-    for condition, _, copy in round_one[:6] + round_one[8:]:
-        pl.when(condition)(copy.start)
+    def begin(*places):
+        for place in places:
+            condition, _, copy = round_one[place]
+            pl.when(condition)(copy.start)
+
+    begin(2, 3, 4)
     tell(4, [(has_before, {"tm": tb - 1})])
     pass_on(0)
+
+    loads[0].wait()
+    loads[1].wait()
+    viscosity = jnp.zeros((4, 8, 128), F32)
+    for label in range(8):
+        viscosity = jnp.where(vclass[...] == label, table[label], viscosity)
+    build_coefficients(viscosity, coef)
+    loads[2].wait()
+    maps = kind_maps(kind)
+    vk_out[0, 0:4] = viscosity[0, 0:4]
+    vk_out[1, 0:4] = viscosity[3, 4:8]
+    vk_out[0, 4:8] = jnp.zeros((4, 128), F32)
+    vk_out[1, 4:8] = jnp.zeros((4, 128), F32)
+    vk_out[0, 8:16] = maps[0]
+    vk_out[1, 8:16] = maps[3]
+    begin(0, 1)
+    for g in range(4):
+        store_mask(maps[g], mask, g + 1)
+    loads[3].wait()
+    loads[4].wait()
+
+    nothing = [jnp.zeros((4, 128), F32)] * 4
+
+    def local(t):
+        now = [f0[c, t] for c in range(4)]
+        base = [forcing[c, t] for c in range(4)]
+        if t > 0:
+            base = [base[c] + f0[c, t - 1] for c in range(3)] + base[3:]
+        for c, value in enumerate(residual(now, nothing, nothing, base, coef[0], coef)):
+            part[c, t] = value
+
+    for t in range(4):
+        local(t)
+    begin(8, 9)
+    for t in range(4, 8):
+        local(t)
+    @pl.when(has_after)
+    def _():
+        pl.semaphore_wait(token_sem.at[4], 1)
+        begin(6, 7)
+
+    begin(10, 11, 5)
 
     def arrive(first, last):
         for _, awaited, copy in round_one[first:last]:
@@ -358,12 +373,6 @@
     loads[5].wait()
     build_bank(bank, lhs)
     pass_on(1)
-
-    @pl.when(has_after)
-    def _():
-        pl.semaphore_wait(token_sem.at[4], 1)
-        for condition, _, copy in round_one[6:8]:
-            pl.when(condition)(copy.start)
 
     first = (lax.rem(tb, 4) * 8).astype(F32) * (1.0 / 1024.0)
 
@@ -438,20 +447,6 @@
     middle((1, 2, 3))
     middle((4, 5, 6, 7))
 
-    arrive(5, 8)
-    units = [[ares[c, g] for c in range(4)] for g in range(4)]
-    old = [e0[c, 0, 0:4] for c in range(3)]
-    extra = face([lcor[c, 4:8] for c in range(4)], old, faces[0], -1.0)
-    units[0] = [units[0][c] + low(extra[c]) for c in range(4)]
-    old = [e0[c, 3, 4:8] for c in range(3)]
-    extra = face([rcor[c, 0:4] for c in range(4)], old, faces[1], 1.0)
-    units[3] = [units[3][c] + high(extra[c]) for c in range(4)]
-    for g, change in enumerate(corrections(units, [1, 2, 3, 4], lhs, mask)):
-        for c in range(3):
-            e1[c, g] = e0[c, g] + change[c]
-
-    middle((0,))
-
 
     def sum_up(rows):
         for c in range(4):
@@ -460,8 +455,6 @@
             fields[0, c, rows] = near
             fields[1, c, rows] = far
             mass[c, rows] = plain * (1.0 / 1024.0)
-
-    sum_up(slice(1, 3))
 
     def beside(pair):
         units = []
@@ -494,8 +487,22 @@
                 for c in range(4):
                     smoothed[c, t, g] = f1[c, t, g] + changes[2 * n + side][c]
 
-    arrive(8, 12)
+    arrive(5, 12)
     beside(range(8))
+
+    units = [[ares[c, g] for c in range(4)] for g in range(4)]
+    old = [e0[c, 0, 0:4] for c in range(3)]
+    extra = face([lcor[c, 4:8] for c in range(4)], old, faces[0], -1.0)
+    units[0] = [units[0][c] + low(extra[c]) for c in range(4)]
+    old = [e0[c, 3, 4:8] for c in range(3)]
+    extra = face([rcor[c, 0:4] for c in range(4)], old, faces[1], 1.0)
+    units[3] = [units[3][c] + high(extra[c]) for c in range(4)]
+    for g, change in enumerate(corrections(units, [1, 2, 3, 4], lhs, mask)):
+        for c in range(3):
+            e1[c, g] = e0[c, g] + change[c]
+
+    middle((0,))
+    sum_up(slice(1, 3))
     ends(range(8))
 
     for g in (0, 3):
@@ -506,24 +513,18 @@
             for c, value in enumerate(face(near, None, faces[side], sign)):
                 edges[side, pl.ds(4 * half + c, 4, stride=8), :] = value
 
-    def edge_piece(side, y, device):
+    core = lax.rem(tb, 2)
+
+    def swap(source, target, n):
         return pltpu.make_async_remote_copy(
-            edges.at[side, pl.ds(8 * y, 8)], recv_e.at[tb], esend_sem.at[side], erecv_sem,
-            device_id=device, device_id_type=MESH,
+            source, target, pair_send.at[n], pair_recv.at[n], device_id=partner, device_id_type=MESH
         )
 
-
-    pass_on(4)
-
-    @pl.when(has_left)
-    def _():
-        for y in range(4):
-            edge_piece(0, y, {"space": sx - 1, "tm": 28 + y}).start()
-
-    @pl.when(has_right)
-    def _():
-        for y in range(4):
-            edge_piece(1, y, {"space": sx + 1, "tm": y}).start()
+    swaps = [
+        swap(edges.at[1 - core], edges_in, 0),
+        swap(parts.at[pl.ds(pl.multiple_of(128 * (1 - core), 128), 128)], parts_in, 1),
+    ]
+    swaps[0].start()
 
     for half in range(2):
         now = [fields[half, c] for c in range(4)]
@@ -541,58 +542,89 @@
                     value = value - high(faces[1] * now[c][3, 4:8])
                 parts[pl.ds(64 * g + row, 8, stride=8), :] = value
 
+    swaps[1].start()
+
     def tile(ref, row):
         return ref.at[pl.ds(pl.multiple_of(row * 8, 8), 8)]
 
+    pass_on(4)
+    swaps[0].wait_recv()
+    edge_sums[...] = edges[core] + edges_in[...]
+    sends_left, sends_right = both(core == 0, has_left), both(core == 1, has_right)
+
+    def edge_piece(y, device):
+        return pltpu.make_async_remote_copy(
+            edge_sums.at[pl.ds(8 * y, 8)], recv_e.at[tb // 2], esend_sem, erecv_sem,
+            device_id=device, device_id_type=MESH,
+        )
+
+    @pl.when(sends_left)
+    def _():
+        for y in range(4):
+            edge_piece(y, {"space": sx - 1, "tm": 28 + y}).start()
+
+    @pl.when(sends_right)
+    def _():
+        for y in range(4):
+            edge_piece(y, {"space": sx + 1, "tm": y}).start()
+
+    swaps[1].wait_recv()
+    sums[...] = parts[pl.ds(pl.multiple_of(128 * core, 128), 128), :] + parts_in[...]
+
     def send(step, carry):
-        k = step // 4
+        k = step // 2
         odd = lax.rem(k, 2)
         dz = 4 + (k // 2) * (1 - odd) - ((k + 1) // 2) * odd
-        column = lax.rem(lax.rem(tb, 16) + 2 * dz, 16)
-        column = column // 2 * 2 + lax.rem(tb + step, 2)
-        peer = lax.rem(tb // 16 + 1 + lax.rem(step // 2, 2), 2) * 16 + column
+        place = lax.rem(column // 2 * 2 + 2 * dz, 16) + lax.rem(step, 2)
+        peer = 16 * core + place
 
         @pl.when(peer != tb)
         def _():
             pltpu.make_async_remote_copy(
-                tile(parts, peer), recv.at[tb], psend_sem, precv_sem,
+                tile(sums, place), recv.at[tb // 2], psend_sem, precv_sem,
                 device_id={"tm": peer}, device_id_type=MESH,
             ).start()
 
         return carry
 
-    lax.fori_loop(0, 32, send, 0)
-    recv[tb] = tile(parts, tb)[...]
+    lax.fori_loop(0, 16, send, 0)
+    keeps = tb // 16 == core
+
+    @pl.when(keeps)
+    def _():
+        recv[tb // 2] = tile(sums, column)[...]
 
     for condition, _, copy in round_one:
         pl.when(condition)(copy.wait_send)
 
-    def sent_edges(side, device):
+    for copy in swaps:
+        copy.wait_send()
+
+    @pl.when(jnp.logical_or(sends_left, sends_right))
+    def _():
         pltpu.make_async_remote_copy(
-            edges.at[side], edges.at[side], esend_sem.at[side], erecv_sem,
-            device_id=device, device_id_type=MESH,
+            edge_sums, edge_sums, esend_sem, erecv_sem, device_id=partner, device_id_type=MESH
         ).wait_send()
 
-    pl.when(has_left)(lambda: sent_edges(0, to_left))
-    pl.when(has_right)(lambda: sent_edges(1, to_right))
-    pieces = pltpu.make_async_remote_copy(
-        recv.at[0:31], recv.at[0:31], psend_sem, precv_sem, device_id=to_after, device_id_type=MESH
-    )
-    pieces.wait_send()
-    pieces.wait_recv()
+    def settle(number):
+        pieces = pltpu.make_async_remote_copy(
+            recv.at[0:number], recv.at[0:number], psend_sem, precv_sem, device_id=partner, device_id_type=MESH
+        )
+        pieces.wait_send()
+        pieces.wait_recv()
+
+    pl.when(keeps)(lambda: settle(15))
+    pl.when(jnp.logical_not(keeps))(lambda: settle(16))
 
     @pl.when(is_edge)
     def _():
         pltpu.make_async_remote_copy(
-            recv_e, recv_e, psend_sem, erecv_sem, device_id=to_after, device_id_type=MESH
+            recv_e, recv_e, psend_sem, erecv_sem, device_id=partner, device_id_type=MESH
         ).wait_recv()
 
     before = jnp.zeros((4, 128), F32)
     for k in range(8):
-        block = (recv[4 * k] + recv[4 * k + 1]) + (recv[4 * k + 2] + recv[4 * k + 3])
-        block = block + (
-            (recv_e[4 * k] + recv_e[4 * k + 1]) + (recv_e[4 * k + 2] + recv_e[4 * k + 3])
-        )
+        block = (recv[2 * k] + recv[2 * k + 1]) + (recv_e[2 * k] + recv_e[2 * k + 1])
         level = block[0:4] + before
         before = block[4:8]
         for c in range(4):
@@ -654,16 +686,22 @@
             pltpu.VMEM((2, 4, 4, 8, 128), F32),
             pltpu.VMEM((256, 128), F32),
             pltpu.VMEM((2, 32, 128), F32),
-            pltpu.VMEM((32, 8, 128), F32),
-            pltpu.VMEM((32, 8, 128), F32),
+            pltpu.VMEM((128, 128), F32),
+            pltpu.VMEM((32, 128), F32),
+            pltpu.VMEM((128, 128), F32),
+            pltpu.VMEM((32, 128), F32),
+            pltpu.VMEM((16, 8, 128), F32),
+            pltpu.VMEM((16, 8, 128), F32),
             dma((6,)),
             dma((12,)),
             dma((12,)),
             dma,
             dma,
-            dma((2,)),
+            dma,
             dma,
             pltpu.SemaphoreType.REGULAR((5,)),
+            dma((2,)),
+            dma((2,)),
         ],
         compiler_params=pltpu.CompilerParams(
             collective_id=0, has_side_effects=True, vmem_limit_bytes=60 * 1024 * 1024

time: 26.9 us -> 26.2 us (0.974)
  Pallas kernels: 26.2 us -> 25.4 us
    pallas_call x1, Pallas kernels: 25.4 us -> 24.6 us  [per_device(): pl.pallas_call(kernel, out_shape=(pltpu.VMEM((4, 8, 4, 8, 128), F32), plt...]
where the time goes in v7:
time: 26.2 us; the launch traced here: 26.1 us
  Pallas kernels  25.4 us (97%)
  between operations  0.64 us (2%)
    pallas_call x1, Pallas kernels, per_device(): pl.pallas_call(kernel, out_shape=(pltpu.VMEM((4, 8, 4, 8, 128), F32), plt...  24.6 us
    pallas_call x1, Pallas kernels, per_device(): pl.pallas_call(store, out_shape=(jax.ShapeDtypeStruct((4, 8, 4, 8, 128),...  0.81 us

profile of v7, /device:TPU:5, one launch (start us, length us, event | category | flops | bytes accessed | tf_op | source)
XLA Modules:
  0.0 26.1 jit_solution(1674200456822338771)
XLA Ops:
  0.6 24.6 %shard_map.77 = (f32[4,8,4,8,128]{4,3,2,1,0:T(8,128)S(1)}, f32[4,8,128]{2,1,0:T(8,128)S(1)}) custom-call(f32[4,8,8,4,128]{4,3,2,1,0:T(4,128)} %init5.1, f32[4,8,4,8,128]{4,3,2,1,0:T(8,128)} %bitcast.4, f32[4,8,4,8,128]{4,3,2,1,0:T(8,128)} %bitcast.5, f32[8]{0:T(128)} %table_in.1, s32[4,8,128]{2,1,0:T(8,128)} %bitcast.6, bf16[4,32,32]{2,1,0:T(8,128)(2,1)} %bank_in.1, ...), custom_call_target="tpu_custom_call" | custom-call | tf_op jit(solution)/shard_map/pallas_call | solution.py:649
  25.3 0.8 %shard_map.78 = (f32[4,8,4,8,128]{4,3,2,1,0:T(8,128)}, f32[4,8,128]{2,1,0:T(8,128)}) custom-call(f32[4,8,4,8,128]{4,3,2,1,0:T(8,128)S(1)} %get-tuple-element.6.smoothed_in, f32[4,8,128]{2,1,0:T(8,128)S(1)} %get-tuple-element.7.coarse_in), custom_call_target="tpu_custom_call" | custom-call | tf_op jit(solution)/shard_map/pallas_call | solution.py:718

commit v8 on v7

--- a/solution.py
+++ b/solution.py
@@ -195,7 +195,7 @@
     init5, init, forc, table_in, vclass_in, bank_in, kind_in,
     smoothed, coarse, table, vclass, bank, kind,
     f0, f1, forcing, part, part2, e0, e1, lp, rp, lp2, rp2, lres, rres, ares, lcor, rcor, vk_out, vk_in,
-    faces, fields, mass, coef, lhs, mask, weighted_f, parts, edges, parts_in, edges_in, sums, edge_sums, recv, recv_e,
+    faces, fields, mass, coef, lhs, mask, weighted_f, parts, edges, parts_in, sums, recv, recv_e,
     load_sem, send_sem, recv_sem, psend_sem, precv_sem, esend_sem, erecv_sem, token_sem, pair_send, pair_recv,
 ):
     sx = lax.axis_index("space")
@@ -513,18 +513,23 @@
             for c, value in enumerate(face(near, None, faces[side], sign)):
                 edges[side, pl.ds(4 * half + c, 4, stride=8), :] = value
 
-    core = lax.rem(tb, 2)
-
-    def swap(source, target, n):
+    def edge_piece(side, y, device):
         return pltpu.make_async_remote_copy(
-            source, target, pair_send.at[n], pair_recv.at[n], device_id=partner, device_id_type=MESH
+            edges.at[side, pl.ds(8 * y, 8)], recv_e.at[tb], esend_sem.at[side], erecv_sem,
+            device_id=device, device_id_type=MESH,
         )
 
-    swaps = [
-        swap(edges.at[1 - core], edges_in, 0),
-        swap(parts.at[pl.ds(pl.multiple_of(128 * (1 - core), 128), 128)], parts_in, 1),
-    ]
-    swaps[0].start()
+    pass_on(4)
+
+    @pl.when(has_left)
+    def _():
+        for y in range(4):
+            edge_piece(0, y, {"space": sx - 1, "tm": 28 + y}).start()
+
+    @pl.when(has_right)
+    def _():
+        for y in range(4):
+            edge_piece(1, y, {"space": sx + 1, "tm": y}).start()
 
     for half in range(2):
         now = [fields[half, c] for c in range(4)]
@@ -542,43 +547,29 @@
                     value = value - high(faces[1] * now[c][3, 4:8])
                 parts[pl.ds(64 * g + row, 8, stride=8), :] = value
 
-    swaps[1].start()
+    core = lax.rem(tb, 2)
+    swap = pltpu.make_async_remote_copy(
+        parts.at[pl.ds(pl.multiple_of(128 * (1 - core), 128), 128)], parts_in, pair_send, pair_recv,
+        device_id=partner, device_id_type=MESH,
+    )
+    swap.start()
 
     def tile(ref, row):
         return ref.at[pl.ds(pl.multiple_of(row * 8, 8), 8)]
 
-    pass_on(4)
-    swaps[0].wait_recv()
-    edge_sums[...] = edges[core] + edges_in[...]
-    sends_left, sends_right = both(core == 0, has_left), both(core == 1, has_right)
-
-    def edge_piece(y, device):
-        return pltpu.make_async_remote_copy(
-            edge_sums.at[pl.ds(8 * y, 8)], recv_e.at[tb // 2], esend_sem, erecv_sem,
-            device_id=device, device_id_type=MESH,
-        )
-
-    @pl.when(sends_left)
-    def _():
-        for y in range(4):
-            edge_piece(y, {"space": sx - 1, "tm": 28 + y}).start()
-
-    @pl.when(sends_right)
-    def _():
-        for y in range(4):
-            edge_piece(y, {"space": sx + 1, "tm": y}).start()
-
-    swaps[1].wait_recv()
+    swap.wait_recv()
     sums[...] = parts[pl.ds(pl.multiple_of(128 * core, 128), 128), :] + parts_in[...]
 
-    def send(step, carry):
+    def send(step, carry, hot):
         k = step // 2
         odd = lax.rem(k, 2)
         dz = 4 + (k // 2) * (1 - odd) - ((k + 1) // 2) * odd
         place = lax.rem(column // 2 * 2 + 2 * dz, 16) + lax.rem(step, 2)
         peer = 16 * core + place
 
-        @pl.when(peer != tb)
+        is_hot = jnp.logical_or(peer < 4, peer >= 28)
+
+        @pl.when(both(peer != tb, is_hot if hot else jnp.logical_not(is_hot)))
         def _():
             pltpu.make_async_remote_copy(
                 tile(sums, place), recv.at[tb // 2], psend_sem, precv_sem,
@@ -587,7 +578,8 @@
 
         return carry
 
-    lax.fori_loop(0, 16, send, 0)
+    lax.fori_loop(0, 16, functools.partial(send, hot=True), 0)
+    lax.fori_loop(0, 16, functools.partial(send, hot=False), 0)
     keeps = tb // 16 == core
 
     @pl.when(keeps)
@@ -597,14 +589,15 @@
     for condition, _, copy in round_one:
         pl.when(condition)(copy.wait_send)
 
-    for copy in swaps:
-        copy.wait_send()
-
-    @pl.when(jnp.logical_or(sends_left, sends_right))
-    def _():
+    swap.wait_send()
+
+    def sent_edges(side):
         pltpu.make_async_remote_copy(
-            edge_sums, edge_sums, esend_sem, erecv_sem, device_id=partner, device_id_type=MESH
+            edges.at[side], edges.at[side], esend_sem.at[side], erecv_sem, device_id=partner, device_id_type=MESH
         ).wait_send()
+
+    pl.when(has_left)(lambda: sent_edges(0))
+    pl.when(has_right)(lambda: sent_edges(1))
 
     def settle(number):
         pieces = pltpu.make_async_remote_copy(
@@ -624,7 +617,10 @@
 
     before = jnp.zeros((4, 128), F32)
     for k in range(8):
-        block = (recv[2 * k] + recv[2 * k + 1]) + (recv_e[2 * k] + recv_e[2 * k + 1])
+        block = recv[2 * k] + recv[2 * k + 1]
+        block = block + (
+            (recv_e[4 * k] + recv_e[4 * k + 1]) + (recv_e[4 * k + 2] + recv_e[4 * k + 3])
+        )
         level = block[0:4] + before
         before = block[4:8]
         for c in range(4):
@@ -687,21 +683,19 @@
             pltpu.VMEM((256, 128), F32),
             pltpu.VMEM((2, 32, 128), F32),
             pltpu.VMEM((128, 128), F32),
-            pltpu.VMEM((32, 128), F32),
             pltpu.VMEM((128, 128), F32),
-            pltpu.VMEM((32, 128), F32),
             pltpu.VMEM((16, 8, 128), F32),
-            pltpu.VMEM((16, 8, 128), F32),
+            pltpu.VMEM((32, 8, 128), F32),
             dma((6,)),
             dma((12,)),
             dma((12,)),
             dma,
             dma,
+            dma((2,)),
+            dma,
+            pltpu.SemaphoreType.REGULAR((5,)),
             dma,
             dma,
-            pltpu.SemaphoreType.REGULAR((5,)),
-            dma((2,)),
-            dma((2,)),
         ],
         compiler_params=pltpu.CompilerParams(
             collective_id=0, has_side_effects=True, vmem_limit_bytes=60 * 1024 * 1024

time: 26.2 us -> 25.7 us (0.981)
  Pallas kernels: 25.4 us -> 25 us
    pallas_call x1, Pallas kernels: 24.6 us -> 24.2 us  [per_device(): pl.pallas_call(kernel, out_shape=(pltpu.VMEM((4, 8, 4, 8, 128), F32), plt...]
where the time goes in v8:
time: 25.7 us; the launch traced here: 25.6 us
  Pallas kernels  25 us (97%)
  between operations  0.64 us (2%)
    pallas_call x1, Pallas kernels, per_device(): pl.pallas_call(kernel, out_shape=(pltpu.VMEM((4, 8, 4, 8, 128), F32), plt...  24.2 us
    pallas_call x1, Pallas kernels, per_device(): pl.pallas_call(store, out_shape=(jax.ShapeDtypeStruct((4, 8, 4, 8, 128),...  0.81 us

profile of v8, /device:TPU:5, one launch (start us, length us, event | category | flops | bytes accessed | tf_op | source)
XLA Modules:
  0.0 25.6 jit_solution(17594000627400074784)
XLA Ops:
  0.6 24.2 %shard_map.77 = (f32[4,8,4,8,128]{4,3,2,1,0:T(8,128)S(1)}, f32[4,8,128]{2,1,0:T(8,128)S(1)}) custom-call(f32[4,8,8,4,128]{4,3,2,1,0:T(4,128)} %init5.1, f32[4,8,4,8,128]{4,3,2,1,0:T(8,128)} %bitcast.4, f32[4,8,4,8,128]{4,3,2,1,0:T(8,128)} %bitcast.5, f32[8]{0:T(128)} %table_in.1, s32[4,8,128]{2,1,0:T(8,128)} %bitcast.6, bf16[4,32,32]{2,1,0:T(8,128)(2,1)} %bank_in.1, ...), custom_call_target="tpu_custom_call" | custom-call | tf_op jit(solution)/shard_map/pallas_call | solution.py:645
  24.8 0.8 %shard_map.78 = (f32[4,8,4,8,128]{4,3,2,1,0:T(8,128)}, f32[4,8,128]{2,1,0:T(8,128)}) custom-call(f32[4,8,4,8,128]{4,3,2,1,0:T(8,128)S(1)} %get-tuple-element.6.smoothed_in, f32[4,8,128]{2,1,0:T(8,128)S(1)} %get-tuple-element.7.coarse_in), custom_call_target="tpu_custom_call" | custom-call | tf_op jit(solution)/shard_map/pallas_call | solution.py:712

commit v9 on v8

--- a/solution.py
+++ b/solution.py
@@ -255,8 +255,11 @@
         pltpu.make_async_copy(forc, forcing, load_sem.at[4]),
         pltpu.make_async_copy(bank_in, bank, load_sem.at[5]),
     ]
-    for copy in loads:
+    for copy in loads[:3] + loads[5:]:
         copy.start()
+    for c in range(4):
+        pltpu.make_async_copy(init.at[c], f0.at[c], load_sem.at[3]).start()
+        pltpu.make_async_copy(forc.at[c], forcing.at[c], load_sem.at[4]).start()
 
     @pl.when(sx == 0)
     def _():
@@ -359,12 +362,13 @@
     begin(8, 9)
     for t in range(4, 8):
         local(t)
+    begin(5)
     @pl.when(has_after)
     def _():
         pl.semaphore_wait(token_sem.at[4], 1)
         begin(6, 7)
 
-    begin(10, 11, 5)
+    begin(10, 11)
 
     def arrive(first, last):
         for _, awaited, copy in round_one[first:last]:

time: 25.7 us -> 25.7 us (level)
  no operation moved by 1% of the time
where the time goes in v9:
time: 25.7 us; the launch traced here: 25.6 us
  Pallas kernels  25 us (97%)
  between operations  0.64 us (2%)
    pallas_call x1, Pallas kernels, per_device(): pl.pallas_call(kernel, out_shape=(pltpu.VMEM((4, 8, 4, 8, 128), F32), plt...  24.2 us
    pallas_call x1, Pallas kernels, per_device(): pl.pallas_call(store, out_shape=(jax.ShapeDtypeStruct((4, 8, 4, 8, 128),...  0.81 us

profile of v9, /device:TPU:5, one launch (start us, length us, event | category | flops | bytes accessed | tf_op | source)
XLA Modules:
  0.0 25.6 jit_solution(3976748301117634299)
XLA Ops:
  0.6 24.2 %shard_map.77 = (f32[4,8,4,8,128]{4,3,2,1,0:T(8,128)S(1)}, f32[4,8,128]{2,1,0:T(8,128)S(1)}) custom-call(f32[4,8,8,4,128]{4,3,2,1,0:T(4,128)} %init5.1, f32[4,8,4,8,128]{4,3,2,1,0:T(8,128)} %bitcast.4, f32[4,8,4,8,128]{4,3,2,1,0:T(8,128)} %bitcast.5, f32[8]{0:T(128)} %table_in.1, s32[4,8,128]{2,1,0:T(8,128)} %bitcast.6, bf16[4,32,32]{2,1,0:T(8,128)(2,1)} %bank_in.1, ...), custom_call_target="tpu_custom_call" | custom-call | tf_op jit(solution)/shard_map/pallas_call | solution.py:649
  24.8 0.8 %shard_map.78 = (f32[4,8,4,8,128]{4,3,2,1,0:T(8,128)}, f32[4,8,128]{2,1,0:T(8,128)}) custom-call(f32[4,8,4,8,128]{4,3,2,1,0:T(8,128)S(1)} %get-tuple-element.6.smoothed_in, f32[4,8,128]{2,1,0:T(8,128)S(1)} %get-tuple-element.7.coarse_in), custom_call_target="tpu_custom_call" | custom-call | tf_op jit(solution)/shard_map/pallas_call | solution.py:716

commit v10 on v9

--- a/solution.py
+++ b/solution.py
@@ -342,8 +342,6 @@
     vk_out[0, 8:16] = maps[0]
     vk_out[1, 8:16] = maps[3]
     begin(0, 1)
-    for g in range(4):
-        store_mask(maps[g], mask, g + 1)
     loads[3].wait()
     loads[4].wait()
 
@@ -369,6 +367,8 @@
         begin(6, 7)
 
     begin(10, 11)
+    for g in range(4):
+        store_mask(maps[g], mask, g + 1)
 
     def arrive(first, last):
         for _, awaited, copy in round_one[first:last]:

time: 25.7 us -> 25.7 us (level)
  no operation moved by 1% of the time
where the time goes in v10:
time: 25.7 us; the launch traced here: 25.6 us
  Pallas kernels  25 us (97%)
  between operations  0.64 us (2%)
    pallas_call x1, Pallas kernels, per_device(): pl.pallas_call(kernel, out_shape=(pltpu.VMEM((4, 8, 4, 8, 128), F32), plt...  24.2 us
    pallas_call x1, Pallas kernels, per_device(): pl.pallas_call(store, out_shape=(jax.ShapeDtypeStruct((4, 8, 4, 8, 128),...  0.81 us

profile of v10, /device:TPU:5, one launch (start us, length us, event | category | flops | bytes accessed | tf_op | source)
XLA Modules:
  0.0 25.6 jit_solution(14800556180029284139)
XLA Ops:
  0.6 24.2 %shard_map.77 = (f32[4,8,4,8,128]{4,3,2,1,0:T(8,128)S(1)}, f32[4,8,128]{2,1,0:T(8,128)S(1)}) custom-call(f32[4,8,8,4,128]{4,3,2,1,0:T(4,128)} %init5.1, f32[4,8,4,8,128]{4,3,2,1,0:T(8,128)} %bitcast.4, f32[4,8,4,8,128]{4,3,2,1,0:T(8,128)} %bitcast.5, f32[8]{0:T(128)} %table_in.1, s32[4,8,128]{2,1,0:T(8,128)} %bitcast.6, bf16[4,32,32]{2,1,0:T(8,128)(2,1)} %bank_in.1, ...), custom_call_target="tpu_custom_call" | custom-call | tf_op jit(solution)/shard_map/pallas_call | solution.py:649
  24.8 0.8 %shard_map.78 = (f32[4,8,4,8,128]{4,3,2,1,0:T(8,128)}, f32[4,8,128]{2,1,0:T(8,128)}) custom-call(f32[4,8,4,8,128]{4,3,2,1,0:T(8,128)S(1)} %get-tuple-element.6.smoothed_in, f32[4,8,128]{2,1,0:T(8,128)S(1)} %get-tuple-element.7.coarse_in), custom_call_target="tpu_custom_call" | custom-call | tf_op jit(solution)/shard_map/pallas_call | solution.py:716
